TPU v7x, 32 devices: a whole 2x2x4 slice. The times are simulated.
32 devices in a mesh: rep: 8 (over y, x, core), tp: 4 (over z).
Axes of the slice: x: 2, y: 2, z: 4, core: 2. Of those that a mesh axis runs over, the one named last changes fastest.
Arguments:
- queries: bfloat16 [8, 4, 16384], P('rep'), may hold values from -18 to 18
- cache_keys: bfloat16 [8, 4, 16, 64, 256], P('rep', 'tp'), may hold values from -8 to 8
- cache_values: bfloat16 [8, 4, 16, 64, 256], P('rep', 'tp'), may hold values from -6 to 6
- page_table: int32 [8, 4, 16], P('rep', 'tp'), may hold values from 0 to 15, each once within a row
- lengths: int32 [8], P('rep'), may hold values from 4 to 1024, as said below
- history: bfloat16 [8, 12, 16384], P('rep', None, 'tp'), may hold values from -10 to 10
- norm_gain: float32 [16384], P('tp'), may hold values from 0.5 to 2
- draft_weight: float32 [16384, 16384], P('tp', 'rep'), may hold values from -0.1640625 to 0.1640625
- targets: int32 [8, 16], replicated, may hold values from 0 to 16383
- accepted: int32 [8], replicated, may hold values from 1 to 16, as said below
Outputs:
- attended: bfloat16 [8, 4, 16384], P('rep', None, 'tp')
- new_weight: float32 [16384, 16384], P('tp', 'rep')
Inputs may be any that keep to these rules, and one draw needn't show every extreme that they name: `lengths`: some replica's sequence has length exactly 1024. `accepted`: some replica trains all 16 rows.
All inputs are finite; a program needn't handle non-finite values.
Results may differ from a plain program's by a relative error of at most 0.01.
Values may be sent and summed in bfloat16 or wider, within the bound.
No kernel may reach another device: no remote copies, remote signals or barrier semaphores. Data moves between devices by JAX's collectives and lax.ppermute only.
A program may use at most 128 MiB of HBM per device.

v0:
```python
import jax
import jax.numpy as jnp
from jax import lax
from jax.sharding import PartitionSpec as P

HQ = 128
KVH = 8
HD = 128
D = 16384


learn_rate = 0.5


def partner_2(value, axis, distance):
    mask = 2**distance
    pairs = [(source, source ^ mask) for source in range(lax.axis_size(axis))]
    return lax.ppermute(value, axis, pairs)


def merged(value, axis, join):
    pieces = jax.tree.map(lambda part: lax.all_gather(part, axis), value)
    head = jax.tree.map(lambda part: part[0], pieces)
    tail = jax.tree.map(lambda part: part[1:], pieces)
    so_far, _ = lax.scan(lambda so_far, share: (join(so_far, share), None), head, tail)
    return so_far


def attend(query, keys, values, position, length, kv_local, group_heads):
    steps = query.shape[0]
    limit = length - steps + jnp.arange(steps, dtype=jnp.int32)
    valid = (position[None, :] <= limit[:, None])[:, None, None, :]
    grouped = query.astype(jnp.float32).reshape(steps, kv_local, group_heads, HD)
    scores = jnp.einsum("skgd,pkd->skgp", grouped, keys.astype(jnp.float32)) * HD ** (-0.5)
    top = jnp.max(jnp.where(valid, scores, -1e30), axis=-1)
    expo = jnp.where(valid, jnp.exp(scores - top[..., None]), 0.0)
    total = jnp.sum(expo, axis=-1)
    weighted = jnp.einsum("skgp,pkd->skgd", expo, values.astype(jnp.float32))
    return (top, total, weighted)


def join_softmax(first, second):
    top = jnp.maximum(first[0], second[0])
    left = jnp.exp(first[0] - top)
    right = jnp.exp(second[0] - top)
    return (
        top,
        first[1] * left + second[1] * right,
        first[2] * left[..., None] + second[2] * right[..., None],
    )


def join_stats(first, second):
    top = jnp.maximum(first[0], second[0])
    return (top, first[1] * jnp.exp(first[0] - top) + second[1] * jnp.exp(second[0] - top))


def on_device(
    queries,
    cache_keys,
    cache_values,
    page_table,
    lengths,
    history,
    norm_gain,
    draft_weight,
    targets,
    accepted,
):
    owner = lax.axis_index("tp")
    owners = lax.axis_size("tp")
    kv_local = cache_keys.shape[4] // HD
    sharing = max(1, owners // KVH)
    group_heads = HQ // KVH
    own_heads = HQ // owners
    segment = owner % sharing
    first_head = owner // sharing * kv_local
    table = page_table[0, 0]
    keys = cache_keys[0, 0][table].reshape(-1, kv_local, HD)
    values = cache_values[0, 0][table].reshape(-1, kv_local, HD)
    pages = table.shape[0]
    slots = cache_keys.shape[3]
    position = (
        (jnp.arange(pages, dtype=jnp.int32)[:, None] * sharing + segment) * slots
        + jnp.arange(slots, dtype=jnp.int32)[None, :]
    ).reshape(-1)
    span = kv_local * group_heads * HD
    query = lax.dynamic_slice_in_dim(queries[0], first_head * group_heads * HD, span, 1)
    state = attend(query, keys, values, position, lengths[0], kv_local, group_heads)
    for section in range(sharing.bit_length() - 1):
        partner = partner_2((state[0], state[1], state[2]), "tp", section)
        state = join_softmax(state, partner)
    top, total, weighted = state
    steps = query.shape[0]
    heads = (weighted / total[..., None]).reshape(steps, kv_local * group_heads, HD)
    chosen = lax.dynamic_slice_in_dim(heads, segment * own_heads, own_heads, 1)
    attended = chosen.reshape(1, steps, own_heads * HD).astype(jnp.bfloat16)
    raw = jnp.concatenate([attended[0], history[0]], axis=0)
    rows_each = raw.shape[0]
    wide = raw.astype(jnp.float32)
    squares = lax.psum(jnp.sum(wide * wide, axis=-1), "tp")
    row_scale = lax.rsqrt(squares / D + 1e-05)
    scaled_rows = wide * row_scale[:, None] * norm_gain
    gathered = lax.all_gather(scaled_rows, "rep", axis=0, tiled=True)
    partial_value = jnp.dot(
        gathered, draft_weight, precision=lax.Precision.HIGHEST, preferred_element_type=jnp.float32
    )
    logits = lax.psum(partial_value, "tp")
    columns = draft_weight.shape[1]
    column_start = lax.axis_index("rep") * columns
    local_top = jnp.max(logits, axis=-1)
    local_total = jnp.sum(jnp.exp(logits - local_top[:, None]), axis=-1)
    top_all, total_all = merged((local_top, local_total), "rep", join_stats)
    probs = jnp.exp(logits - top_all[:, None]) / total_all[:, None]
    labels = column_start + jnp.arange(columns, dtype=jnp.int32)
    onehot = (targets.reshape(-1)[:, None] == labels[None, :]).astype(jnp.float32)
    keep = (
        (jnp.arange(rows_each, dtype=jnp.int32)[None, :] < accepted[:, None])
        .reshape(-1)
        .astype(jnp.float32)
    )
    delta = (probs - onehot) * keep[:, None]
    grad = jnp.dot(
        gathered.T, delta, precision=lax.Precision.HIGHEST, preferred_element_type=jnp.float32
    )
    return (attended, draft_weight - learn_rate * grad)


def solution(mesh):
    return jax.shard_map(
        on_device,
        mesh=mesh,
        in_specs=(
            P("rep", None, None),
            P("rep", "tp", None, None, None),
            P("rep", "tp", None, None, None),
            P("rep", "tp", None),
            P("rep"),
            P("rep", None, "tp"),
            P("tp"),
            P("tp", "rep"),
            P(),
            P(),
        ),
        out_specs=(P("rep", None, "tp"), P("tp", "rep")),
        check_vma=False,
    )
```

profile of v0, /device:TPU:0, one launch (start us, length us, event | category | flops | bytes accessed | tf_op | source)
XLA Modules:
  0.0 196.2 jit_solution(16403845232501393093)
XLA Ops:
  7.2 0.0 all-gather.6.cloned.1.call-start
  8.0 0.7 fusion.30
  8.6 0.1 iota_add_fusion.1
  8.7 0.1 add.81
  8.8 0.8 dynamic-slice_bitcast_fusion
  9.6 0.6 gather_fusion.1
  10.2 0.1 reshape.140
  10.3 1.6 gather_fusion
  11.9 0.1 reshape.139
  12.1 0.1 broadcast_compare_fusion
  12.1 0.4 select_reduce_fusion
  12.5 0.2 fusion.22
  12.8 0.3 fusion.7
  13.1 1.1 fusion.23
  14.2 13.5 %psum.14 = f32[16]{0:T(128)S(1)} all-reduce(f32[16]{0:T(128)S(1)} %fusion.23), channel_id=1, replica_groups=mesh['rep'=8,'tp'=4] {'tp'}, use_global_device_ids=true, to_apply=%region_3.4 | all-reduce | flops 16 | bytes 128 | tf_op jit(solution)/shard_map/psum | solution.py:101
  27.7 1.7 fusion.24
  29.4 0.0 all-gather.6.cloned.1.call-update
  29.4 0.0 all-reduce.2.cloned.1.call-start
  29.4 26.2 %all-gather.6.cloned.1.call-done = f32[128,4096]{1,0:T(8,128)} async-done(((f32[16,4096]{1,0:T(8,128)}), f32[128,4096]{1,0:T(8,128)}) %all-gather.6.cloned.1.call-update) | async-done | bytes 2097168 | tf_op jit(solution)/shard_map/all_gather | solution.py:104
  55.7 25.8 %fusion.33 = f32[128,2048]{1,0:T(8,128)} fusion(f32[128,4096]{1,0:T(8,128)} %all-gather.6.cloned.1.call-done, f32[4096,2048]{1,0:T(8,128)} %param.19), kind=kOutput, calls=%fused_computation.60 | convolution fusion | flops 12884901888 | bytes 36700160 | tf_op jit(solution)/shard_map/dot_general | solution.py:105
  81.5 0.0 all-reduce.2.cloned.1.call-update
  81.5 0.6 convert_element_type.38
  82.1 0.1 eq.17
  82.2 0.1 fusion.29
  82.3 0.1 reshape.142
  82.4 51.1 %all-reduce.2.cloned.1.call-done = f32[128,2048]{1,0:T(8,128)} async-done(((f32[128,2048]{1,0:T(8,128)}), f32[128,2048]{1,0:T(8,128)}) %all-reduce.2.cloned.1.call-update) | async-done | bytes 1048592 | tf_op jit(solution)/shard_map/psum | solution.py:108
  133.5 1.4 reduce_max.19
  134.8 1.5 exponential_reduce_fusion
  136.3 8.7 %all-gather.3 = f32[8,1,128]{2,1,0:T(1,128)S(1)} all-gather(f32[1,1,128]{2,1,0:T(1,128)S(1)} %bitcast.73), channel_id=3, replica_groups=mesh['rep'=8,'tp'=4] {'rep'}, dimensions={0}, use_global_device_ids=true | all-gather | bytes 4608 | tf_op jit(solution)/shard_map/all_gather | solution.py:22
  145.1 8.9 %all-gather.2 = f32[8,1,128]{2,1,0:T(1,128)S(1)} all-gather(f32[1,1,128]{2,1,0:T(1,128)S(1)} %bitcast.72), channel_id=2, replica_groups=mesh['rep'=8,'tp'=4] {'rep'}, dimensions={0}, use_global_device_ids=true | all-gather | bytes 4608 | tf_op jit(solution)/shard_map/all_gather | solution.py:22
  153.9 0.3 while.12
  154.2 35.1 %multiply_subtract_fusion = f32[4096,2048]{1,0:T(8,128)} fusion(f32[4096,2048]{1,0:T(8,128)} %param.19, f32[128,4096]{1,0:T(8,128)S(1)} %copy-done.1, f32[128,2048]{1,0:T(8,128)} %all-reduce.2.cloned.1.call-done, f32[128]{0:T(128)S(1)} %reshape.142, s32[2048]{0:T(1024)S(1)} %iota_add_fusion, f32[128]{0:T(128)S(1)} %get-tuple-element.31, ...), kind=kOutput, calls=%fused_computation.9 | convolution fusion | flops 12903251968 | bytes 70264832 | tf_op jit(solution)/shard_map/dot_general | solution.py:123
  (29 shorter events, 0.3 us)
Async XLA Ops:
  7.2 2.4 %copy-start = (bf16[1,1,16,64,256]{4,3,2,1,0:T(8,128)(2,1)S(1)}, bf16[1,1,16,64,256]{4,3,2,1,0:T(8,128)(2,1)}, u32[]{:S(2)}) copy-start(bf16[1,1,16,64,256]{4,3,2,1,0:T(8,128)(2,1)} %param.13) | copy-start | bytes 1572868
  7.2 74.9 %copy-start.2 = (s32[8,16]{1,0:T(8,128)S(1)}, s32[8,16]{1,0:T(8,128)}, u32[]{:S(2)}) copy-start(s32[8,16]{1,0:T(8,128)} %param.20) | copy-start | bytes 1540
  7.2 75.0 %copy-start.3 = (s32[8]{0:T(128)S(1)}, s32[8]{0:T(128)}, u32[]{:S(2)}) copy-start(s32[8]{0:T(128)} %param.21) | copy-start | bytes 100
  7.2 48.5 %all-gather.6.cloned.1.call-start = ((), (), s32[]{:S(2)}) async-start(), calls=%async_computation | async-start | bytes 2359296 | tf_op jit(solution)/shard_map/all_gather | solution.py:104
  29.4 104.1 %all-reduce.2.cloned.1.call-start = ((), (), s32[]{:S(2)}) async-start(), calls=%async_computation.1 | async-start | bytes 2097152 | tf_op jit(solution)/shard_map/psum | solution.py:108
  55.7 98.6 %copy-start.1 = (f32[128,4096]{1,0:T(8,128)S(1)}, f32[128,4096]{1,0:T(8,128)}, u32[]{:S(2)}) copy-start(f32[128,4096]{1,0:T(8,128)} %all-gather.6.cloned.1.call-done) | copy-start | bytes 6291460
Sparse Core Ops, SparseCore 0:
  29.5 26.0 all-gather.5
  81.6 51.8 all-reduce.1
where the time goes:
time: 197 us; the launch traced here: 196 us
  waiting for transfers between devices  77.3 us (39%)
  matrix products  61.6 us (31%)
  blocking collectives  31 us (16%)
  between operations  14.9 us (8%)
  other arithmetic  7.01 us (4%)
  local copies, waits for them, and re-layouts  4.15 us (2%)
    psum x1, waiting for transfers between devices, on_device(): logits = lax.psum(partial_value, 'tp')  51.1 us
    dot_general x1, matrix products, on_device(): jnp.dot(gathered.T, delta, precision=lax.Precision.HIGHEST, preferred_ele...  35.1 us
    all_gather x1, waiting for transfers between devices, on_device(): gathered = lax.all_gather(scaled_rows, 'rep', axis=0, tiled=True)  26.2 us
    dot_general x1, matrix products, on_device(): jnp.dot(gathered, draft_weight, precision=lax.Precision.HIGHEST, preferre...  25.8 us
    all_gather x2, blocking collectives, merged(): pieces = jax.tree.map(lambda part: lax.all_gather(part, axis), value)  17.6 us
    psum x1, blocking collectives, on_device(): squares = lax.psum(jnp.sum(wide * wide, axis=-1), 'tp')  13.5 us
  transfers between devices with their start and end apart: 2, of which 2 were waited for; matrix products, arithmetic and copies ran while one was open for 0% of the time, Pallas kernels for 0%

commit v1 on v0

--- a/solution.py
+++ b/solution.py
@@ -1,6 +1,10 @@
+import functools
+
 import jax
 import jax.numpy as jnp
 from jax import lax
+from jax.experimental import pallas as pl
+from jax.experimental.pallas import tpu as pltpu
 from jax.sharding import PartitionSpec as P
 
 HQ = 128
@@ -8,8 +12,15 @@
 HD = 128
 D = 16384
 
-
 learn_rate = 0.5
+LANES = 128
+MIB = 1024 * 1024
+TILE = 512
+HEIGHT = 256
+HELD = (512, 1024)
+AGAIN = (1024, 512)
+bf16 = jnp.bfloat16
+f32 = jnp.float32
 
 
 def partner_2(value, axis, distance):
@@ -30,12 +41,12 @@
     steps = query.shape[0]
     limit = length - steps + jnp.arange(steps, dtype=jnp.int32)
     valid = (position[None, :] <= limit[:, None])[:, None, None, :]
-    grouped = query.astype(jnp.float32).reshape(steps, kv_local, group_heads, HD)
-    scores = jnp.einsum("skgd,pkd->skgp", grouped, keys.astype(jnp.float32)) * HD ** (-0.5)
+    grouped = query.astype(f32).reshape(steps, kv_local, group_heads, HD)
+    scores = jnp.einsum("skgd,pkd->skgp", grouped, keys.astype(f32)) * HD ** (-0.5)
     top = jnp.max(jnp.where(valid, scores, -1e30), axis=-1)
     expo = jnp.where(valid, jnp.exp(scores - top[..., None]), 0.0)
     total = jnp.sum(expo, axis=-1)
-    weighted = jnp.einsum("skgp,pkd->skgd", expo, values.astype(jnp.float32))
+    weighted = jnp.einsum("skgp,pkd->skgd", expo, values.astype(f32))
     return (top, total, weighted)
 
 
@@ -55,7 +66,7 @@
     return (top, first[1] * jnp.exp(first[0] - top) + second[1] * jnp.exp(second[0] - top))
 
 
-def on_device(
+def general_plan(
     queries,
     cache_keys,
     cache_values,
@@ -94,16 +105,16 @@
     steps = query.shape[0]
     heads = (weighted / total[..., None]).reshape(steps, kv_local * group_heads, HD)
     chosen = lax.dynamic_slice_in_dim(heads, segment * own_heads, own_heads, 1)
-    attended = chosen.reshape(1, steps, own_heads * HD).astype(jnp.bfloat16)
+    attended = chosen.reshape(1, steps, own_heads * HD).astype(bf16)
     raw = jnp.concatenate([attended[0], history[0]], axis=0)
     rows_each = raw.shape[0]
-    wide = raw.astype(jnp.float32)
+    wide = raw.astype(f32)
     squares = lax.psum(jnp.sum(wide * wide, axis=-1), "tp")
     row_scale = lax.rsqrt(squares / D + 1e-05)
     scaled_rows = wide * row_scale[:, None] * norm_gain
     gathered = lax.all_gather(scaled_rows, "rep", axis=0, tiled=True)
     partial_value = jnp.dot(
-        gathered, draft_weight, precision=lax.Precision.HIGHEST, preferred_element_type=jnp.float32
+        gathered, draft_weight, precision=lax.Precision.HIGHEST, preferred_element_type=f32
     )
     logits = lax.psum(partial_value, "tp")
     columns = draft_weight.shape[1]
@@ -113,22 +124,701 @@
     top_all, total_all = merged((local_top, local_total), "rep", join_stats)
     probs = jnp.exp(logits - top_all[:, None]) / total_all[:, None]
     labels = column_start + jnp.arange(columns, dtype=jnp.int32)
-    onehot = (targets.reshape(-1)[:, None] == labels[None, :]).astype(jnp.float32)
+    onehot = (targets.reshape(-1)[:, None] == labels[None, :]).astype(f32)
     keep = (
         (jnp.arange(rows_each, dtype=jnp.int32)[None, :] < accepted[:, None])
         .reshape(-1)
-        .astype(jnp.float32)
+        .astype(f32)
     )
     delta = (probs - onehot) * keep[:, None]
-    grad = jnp.dot(
-        gathered.T, delta, precision=lax.Precision.HIGHEST, preferred_element_type=jnp.float32
+    grad = jnp.dot(gathered.T, delta, precision=lax.Precision.HIGHEST, preferred_element_type=f32)
+    return (attended, draft_weight - learn_rate * grad)
+
+
+def exchange(value, axis, mask):
+    pairs = [(source, source ^ mask) for source in range(lax.axis_size(axis))]
+    return lax.ppermute(value, axis, pairs)
+
+
+def whole(space=pltpu.VMEM):
+    return pl.BlockSpec(memory_space=space)
+
+
+def in_hbm(value):
+    return pltpu.with_memory_space_constraint(value, pltpu.HBM)
+
+
+def attention_kernel(
+    kv_local,
+    table_ref,
+    length_ref,
+    queries_ref,
+    keys_ref,
+    values_ref,
+    history_ref,
+    weight_ref,
+    raw_ref,
+    attended_ref,
+    held_ref,
+    query_buf,
+    key_buf,
+    value_buf,
+    history_buf,
+    query_sem,
+    key_sem,
+    value_sem,
+    history_sem,
+    weight_sem,
+):
+    pages, slots = keys_ref.shape[0], keys_ref.shape[1]
+    steps = query_buf.shape[0]
+    group = HQ // KVH
+    span = query_buf.shape[1]
+    start = pl.multiple_of(lax.axis_index("tp") * span, span)
+    query_copy = pltpu.make_async_copy(queries_ref.at[:, pl.ds(start, span)], query_buf, query_sem)
+    query_copy.start()
+    key_copies, value_copies = [], []
+    for source, target, sems, copies in (
+        (keys_ref, key_buf, key_sem, key_copies),
+        (values_ref, value_buf, value_sem, value_copies),
+    ):
+        for page in range(pages):
+            copy = pltpu.make_async_copy(
+                source.at[table_ref[page]], target.at[pl.ds(page * slots, slots)], sems.at[page]
+            )
+            copy.start()
+            copies.append(copy)
+    history_copy = pltpu.make_async_copy(history_ref, history_buf, history_sem)
+    history_copy.start()
+    query_copy.wait()
+    queries = query_buf[...].astype(f32)
+    stacked = []
+    for head in range(kv_local):
+        parts = [
+            queries[:, (head * group + g) * HD : (head * group + g + 1) * HD] for g in range(group)
+        ]
+        stacked.append(jnp.concatenate(parts, axis=0).astype(bf16))
+    for copy in key_copies + value_copies:
+        copy.wait()
+    weight_copies = column_copies(weight_ref, held_ref, weight_sem, 0)
+    for copy in weight_copies:
+        copy.start()
+    shape = (group * steps, pages * slots)
+    step = lax.broadcasted_iota(jnp.int32, shape, 0) % steps
+    position = lax.broadcasted_iota(jnp.int32, shape, 1)
+    valid = position <= length_ref[0] - steps + step
+    expos, totals = [], []
+    for head in range(kv_local):
+        scores = lax.dot_general(
+            stacked[head],
+            key_buf[:, head * HD : (head + 1) * HD],
+            (((1,), (1,)), ((), ())),
+            preferred_element_type=f32,
+        ) * (HD ** (-0.5))
+        top = jnp.max(jnp.where(valid, scores, -1e30), axis=-1, keepdims=True)
+        expo = jnp.where(valid, jnp.exp(scores - top), 0.0)
+        totals.append(jnp.sum(expo, axis=-1, keepdims=True))
+        expos.append(jnp.concatenate(split2(expo), axis=0))
+    history_copy.wait()
+    for head in range(kv_local):
+        both = jnp.dot(
+            expos[head],
+            value_buf[:, head * HD : (head + 1) * HD],
+            preferred_element_type=f32,
+        )
+        half = group * steps
+        out = (both[:half] + both[half:]) / totals[head]
+        for g in range(group):
+            columns = slice((head * group + g) * HD, (head * group + g + 1) * HD)
+            piece = out[g * steps : (g + 1) * steps]
+            earlier = history_buf[:, columns].astype(f32)
+            raw_ref[:, columns] = jnp.concatenate([piece, earlier], axis=0).astype(bf16)
+            attended_ref[:, columns] = piece.astype(bf16)
+    for copy in weight_copies:
+        copy.wait()
+
+
+def run_attention(queries, keys, values, table, length, history, weight, held):
+    pages, slots, width = keys.shape
+    kv_local = width // HD
+    steps = queries.shape[0]
+    span = kv_local * (HQ // KVH) * HD
+    rows = steps + history.shape[0]
+    return pl.pallas_call(
+        functools.partial(attention_kernel, kv_local),
+        out_shape=(
+            jax.ShapeDtypeStruct((rows, span), bf16),
+            jax.ShapeDtypeStruct((steps, span), bf16),
+            pltpu.VMEM((weight.shape[0], held), f32),
+        ),
+        in_specs=[
+            whole(pltpu.SMEM),
+            whole(pltpu.SMEM),
+            whole(pltpu.HBM),
+            whole(pltpu.HBM),
+            whole(pltpu.HBM),
+            whole(pltpu.HBM),
+            whole(pltpu.HBM),
+        ],
+        out_specs=(whole(), whole(), whole()),
+        scratch_shapes=[
+            pltpu.VMEM((steps, span), bf16),
+            pltpu.VMEM((pages * slots, width), bf16),
+            pltpu.VMEM((pages * slots, width), bf16),
+            pltpu.VMEM(history.shape, bf16),
+            pltpu.SemaphoreType.DMA,
+            pltpu.SemaphoreType.DMA((pages,)),
+            pltpu.SemaphoreType.DMA((pages,)),
+            pltpu.SemaphoreType.DMA,
+            pltpu.SemaphoreType.DMA((held // 256,)),
+        ],
+        compiler_params=pltpu.CompilerParams(vmem_limit_bytes=12 * MIB),
+        cost_estimate=pl.CostEstimate(
+            flops=4 * 64 * 1024 * 256, bytes_accessed=12 * MIB, transcendentals=131072
+        ),
+        name="attention",
+    )(table, length, *(in_hbm(part) for part in (queries, keys, values, history, weight)))
+
+
+def column_copies(source, target, sems, first, width=256):
+    return [
+        pltpu.make_async_copy(
+            source.at[:, pl.ds(first + place, width)],
+            target.at[:, pl.ds(place, width)],
+            sems.at[index],
+        )
+        for index, place in enumerate(range(0, target.shape[1], width))
+    ]
+
+
+def load_kernel(first, count, weight_ref, token_ref, *refs):
+    held_refs, done_ref, sems = refs[:count], refs[count], refs[count + 1]
+    done_ref[...] = jnp.zeros(done_ref.shape, f32)
+    copies = []
+    for ref in held_refs:
+        tiles = len(copies)
+        copies += column_copies(weight_ref, ref, sems.at[pl.ds(tiles, ref.shape[1] // 256)], first)
+        first += ref.shape[1]
+    for copy in copies:
+        copy.start()
+    for copy in copies:
+        copy.wait()
+
+
+def run_load(weight, token, first, widths):
+    rows = weight.shape[0]
+    columns = sum(widths)
+    *helds, done = pl.pallas_call(
+        functools.partial(load_kernel, first, len(widths)),
+        out_shape=tuple(pltpu.VMEM((rows, width), f32) for width in widths)
+        + (jax.ShapeDtypeStruct((8, LANES), f32),),
+        in_specs=[whole(pltpu.HBM), whole(pl.ANY)],
+        out_specs=tuple(whole() for _ in range(len(widths) + 1)),
+        scratch_shapes=[pltpu.SemaphoreType.DMA((columns // 256,))],
+        compiler_params=pltpu.CompilerParams(vmem_limit_bytes=8 * MIB),
+        cost_estimate=pl.CostEstimate(
+            flops=0, bytes_accessed=4 * rows * columns, transcendentals=0
+        ),
+        name="load_weight",
+    )(in_hbm(weight), token)
+    return [pltpu.with_memory_space_constraint(held, pltpu.VMEM) for held in helds], done
+
+
+def split2(value):
+    high = value.astype(bf16)
+    return high, (value - high.astype(f32)).astype(bf16)
+
+
+def stack_kernel(*refs):
+    each = refs[0].shape[0]
+    for k, ref in enumerate(refs[:-2]):
+        refs[-1][k * each : (k + 1) * each, :] = ref[...]
+
+
+def run_stack(parts, after):
+    each, features = parts[0].shape
+    return pl.pallas_call(
+        stack_kernel,
+        out_shape=jax.ShapeDtypeStruct((len(parts) * each, features), bf16),
+        in_specs=[whole() for _ in parts] + [whole(pl.ANY)],
+        out_specs=whole(),
+        compiler_params=pltpu.CompilerParams(vmem_limit_bytes=4 * MIB),
+        cost_estimate=pl.CostEstimate(flops=4096, bytes_accessed=4096, transcendentals=0),
+        name="stacked_rows",
+    )(*parts, after)
+
+
+def power_above(value):
+    exponent = jnp.full(value.shape, -96.0, f32)
+    for step in (128.0, 64.0, 32.0, 16.0, 8.0, 4.0, 2.0, 1.0):
+        exponent = jnp.where(value > jnp.exp2(exponent + (step - 1.0)), exponent + step, exponent)
+    return exponent
+
+
+def logits_kernel(n_rep, n_tp, *refs):
+    block_refs = refs[:2]
+    gain_ref, *held_refs, weight_ref = refs[2:6]
+    x_ref, own_ref, square_ref = refs[6:9]
+    send_refs = refs[9 : 8 + n_tp]
+    scaled_buf, partial_buf, rest_buf, rest_sem = refs[8 + n_tp :]
+    tile = pl.program_id(0)
+    rep, tp = lax.axis_index("rep"), lax.axis_index("tp")
+    rows = x_ref.shape[0]
+    each = rows // n_rep
+    share = rows // n_tp
+    width = partial_buf.shape[1] // pl.num_programs(0)
+    held_columns = sum(ref.shape[1] for ref in held_refs)
+    copies = column_copies(weight_ref, rest_buf, rest_sem, held_columns, width)
+
+    @pl.when(tile == 0)
+    def _():
+        for copy in copies:
+            copy.start()
+        for k in range(n_rep):
+            block = block_refs[k % 2][k // 2 * each : (k // 2 + 1) * each, :]
+            place = pl.multiple_of(lax.bitwise_xor(rep, k) * each, each)
+            x_ref[pl.ds(place, each), :] = block
+            value = block.astype(f32)
+            squares = jnp.sum(value * value, axis=-1, keepdims=True)
+            square_ref[pl.ds(place, each), :] = jnp.broadcast_to(squares, (each, LANES))
+            scaled_buf[pl.ds(place, each), :] = (value * gain_ref[...]).astype(bf16)
+
+    columns = pl.ds(pl.multiple_of(tile * width, width), width)
+
+    def multiply(weight):
+        partial_buf[:, columns] = jnp.dot(
+            scaled_buf[...], weight.astype(bf16), preferred_element_type=f32
+        )
+
+    first = 0
+    for ref in held_refs:
+        for index in range(ref.shape[1] // width):
+
+            @pl.when(tile == first + index)
+            def _():
+                multiply(ref[:, index * width : (index + 1) * width])
+
+        first += ref.shape[1] // width
+    for index, copy in enumerate(copies):
+
+        @pl.when(tile == first + index)
+        def _():
+            copy.wait()
+            multiply(rest_buf[:, index * width : (index + 1) * width])
+
+    @pl.when(tile == pl.num_programs(0) - 1)
+    def _():
+        own_ref[...] = partial_buf[pl.ds(pl.multiple_of(tp * share, share), share), :]
+        full = partial_buf.shape[1]
+        lane = lax.broadcasted_iota(jnp.int32, (share, LANES), 1)
+        squares = jnp.zeros((share, LANES), f32)
+        group = LANES // n_tp
+        for j in range(n_tp):
+            mine = (lane >= j * group) & (lane < (j + 1) * group)
+            squares = jnp.where(mine, square_ref[j * share : (j + 1) * share, :], squares)
+        first = jnp.floor(squares / 16.0)
+        second = jnp.floor((squares - first * 16.0) * 2048.0)
+        third = jnp.floor((squares - first * 16.0 - second / 2048.0) * 2.0**26)
+        part = lane % group
+        extra = jnp.where(part == 0, first, jnp.where(part == 1, second, third))
+        for k in range(1, n_tp):
+            place = pl.multiple_of(lax.bitwise_xor(tp, k) * share, share)
+            value = partial_buf[pl.ds(place, share), :]
+            exponent = power_above(jnp.max(jnp.abs(value), axis=-1, keepdims=True))
+            coded = jnp.floor(value * jnp.exp2(15.0 - exponent) + 0.5)
+            coded = jnp.clip(coded, -32768.0, 32767.0)
+            send_refs[k - 1][:, :full] = coded.astype(jnp.int32).astype(jnp.int16)
+            tail = jnp.where(part == 3, exponent, extra)
+            send_refs[k - 1][:, full:] = tail.astype(jnp.int32).astype(jnp.int16)
+
+
+def run_logits(blocks, gain, helds, weight, n_rep, n_tp):
+    rows, features = 2 * blocks[0].shape[0], blocks[0].shape[1]
+    columns = weight.shape[1]
+    share = rows // n_tp
+    tiles = columns // TILE
+    rest = columns - sum(held.shape[1] for held in helds)
+    return pl.pallas_call(
+        functools.partial(logits_kernel, n_rep, n_tp),
+        grid=(tiles,),
+        out_shape=(
+            jax.ShapeDtypeStruct((rows, features), bf16),
+            jax.ShapeDtypeStruct((share, columns), f32),
+            jax.ShapeDtypeStruct((rows, LANES), f32),
+        )
+        + tuple(
+            jax.ShapeDtypeStruct((share, columns + LANES), jnp.int16) for _ in range(n_tp - 1)
+        ),
+        in_specs=[whole() for _ in range(3 + len(helds))] + [whole(pltpu.HBM)],
+        out_specs=tuple(whole() for _ in range(n_tp + 2)),
+        scratch_shapes=[
+            pltpu.VMEM((rows, features), bf16),
+            pltpu.VMEM((rows, columns), f32),
+            pltpu.VMEM((features, rest), f32),
+            pltpu.SemaphoreType.DMA((rest // TILE,)),
+        ],
+        compiler_params=pltpu.CompilerParams(vmem_limit_bytes=14 * MIB),
+        cost_estimate=pl.CostEstimate(
+            flops=6 * rows * features * columns,
+            bytes_accessed=4 * features * columns,
+            transcendentals=0,
+        ),
+        name="partial_logits",
+    )(*blocks, gain, *helds, in_hbm(weight))
+
+
+def decoded(ref, columns):
+    share = ref.shape[0]
+    tail = ref[:, columns:].astype(jnp.int32).astype(f32)
+    part = lax.broadcasted_iota(jnp.int32, (share, LANES), 1) % (LANES // lax.axis_size("tp"))
+    unit = jnp.where(part == 0, 16.0, jnp.where(part == 1, 1.0 / 2048.0, 2.0**-26))
+    unit = jnp.where(part < 3, unit, 0.0)
+    value = ref[:, :columns].astype(jnp.int32).astype(f32)
+    return value * jnp.exp2(tail[:, 3:4] - 15.0), tail * unit
+
+
+def first_sum_kernel(own_ref, received_ref, sum_ref, square_ref):
+    value, squares = decoded(received_ref, own_ref.shape[1])
+    sum_ref[...] = own_ref[...] + value
+    square_ref[...] = squares
+
+
+def run_first_sum(own, received):
+    share, columns = own.shape
+    return pl.pallas_call(
+        first_sum_kernel,
+        out_shape=(
+            jax.ShapeDtypeStruct((share, columns), f32),
+            jax.ShapeDtypeStruct((share, LANES), f32),
+        ),
+        in_specs=[whole(), whole()],
+        out_specs=(whole(), whole()),
+        compiler_params=pltpu.CompilerParams(vmem_limit_bytes=8 * MIB),
+        cost_estimate=pl.CostEstimate(flops=65536, bytes_accessed=65536, transcendentals=0),
+        name="first_sum",
+    )(own, received)
+
+
+def softmax_kernel(n_tp, n_more, sum_ref, square_ref, first_ref, *refs):
+    received = refs[: n_tp - 2]
+    expo_ref, scale_ref = refs[n_tp - 2 + n_more : n_tp + n_more]
+    share, columns = sum_ref.shape
+    group = LANES // n_tp
+    lane = lax.broadcasted_iota(jnp.int32, (share, LANES), 1)
+    logits, squares = sum_ref[...], first_ref[...]
+    for ref in received:
+        value, more = decoded(ref, columns)
+        logits, squares = logits + value, squares + more
+    for j in range(n_tp):
+        rows = slice(j * share, (j + 1) * share)
+        mine = jnp.where((lane >= j * group) & (lane < (j + 1) * group), squares, 0.0)
+        total = square_ref[rows, :] + jnp.sum(mine, axis=-1, keepdims=True)
+        scale_ref[rows, :] = lax.rsqrt(total / D + 1e-05)
+    tp = lax.axis_index("tp")
+    scale = scale_ref[pl.ds(pl.multiple_of(tp * share, share), share), :]
+    logits = logits * scale[:, :1]
+    top = jnp.max(logits, axis=-1, keepdims=True)
+    expo = jnp.exp(logits - top)
+    total = jnp.sum(expo, axis=-1, keepdims=True)
+    expo_ref[:, :columns] = expo.astype(bf16)
+    for first, value in ((0, top), (3, total)):
+        for place in range(first, first + 3):
+            high = value.astype(bf16)
+            expo_ref[:, columns + place : columns + place + 1] = high
+            value = value - high.astype(f32)
+
+
+def held_shapes(helds):
+    return tuple(pltpu.VMEM(held.shape, f32) for held in helds)
+
+
+def run_softmax(partly, squares, first, received, after, helds):
+    share, columns = partly.shape
+    rows = squares.shape[0]
+    return pl.pallas_call(
+        functools.partial(softmax_kernel, len(received) + 2, len(after) + len(helds)),
+        out_shape=(
+            jax.ShapeDtypeStruct((share, columns + LANES), bf16),
+            jax.ShapeDtypeStruct((rows, LANES), f32),
+        )
+        + held_shapes(helds),
+        in_specs=[whole() for _ in range(len(received) + 3)] + [whole(pl.ANY) for _ in after]
+        + [whole() for _ in helds],
+        out_specs=tuple(whole() for _ in range(2 + len(helds))),
+        input_output_aliases={len(received) + len(after) + 3 + i: 2 + i for i in range(len(helds))},
+        compiler_params=pltpu.CompilerParams(vmem_limit_bytes=8 * MIB),
+        cost_estimate=pl.CostEstimate(flops=65536, bytes_accessed=65536, transcendentals=0),
+        name="local_softmax",
+    )(partly, squares, first, *received, *after, *helds)
+
+
+def stats_kernel(n_tp, n_held, *refs):
+    stats, out_ref, column_buf = refs[:n_tp], refs[n_tp + n_held], refs[-1]
+    share = stats[0].shape[0]
+    tp = lax.axis_index("tp")
+    lane = lax.broadcasted_iota(jnp.int32, (share, LANES), 1)
+    for k, ref in enumerate(stats):
+        parts = ref[:, ref.shape[1] - LANES :].astype(f32)
+        top = parts[:, 0:1] + parts[:, 1:2] + parts[:, 2:3]
+        total = parts[:, 3:4] + parts[:, 4:5] + parts[:, 5:6]
+        place = pl.multiple_of(lax.bitwise_xor(tp, k) * share, share)
+        column_buf[pl.ds(place, share), :] = jnp.where(lane == 0, top, total)
+    out_ref[...] = column_buf[...].T[:8, :]
+
+
+def run_stats(lefts, helds):
+    rows = len(lefts) * lefts[0].shape[0]
+    return pl.pallas_call(
+        functools.partial(stats_kernel, len(lefts), len(helds)),
+        out_shape=(jax.ShapeDtypeStruct((8, rows), f32),) + held_shapes(helds),
+        in_specs=[whole() for _ in range(len(lefts) + len(helds))],
+        out_specs=tuple(whole() for _ in range(1 + len(helds))),
+        input_output_aliases={len(lefts) + i: 1 + i for i in range(len(helds))},
+        scratch_shapes=[pltpu.VMEM((rows, LANES), f32)],
+        compiler_params=pltpu.CompilerParams(vmem_limit_bytes=8 * MIB),
+        cost_estimate=pl.CostEstimate(flops=65536, bytes_accessed=65536, transcendentals=0),
+        name="row_stats",
+    )(*lefts, *helds)
+
+
+def joined(stats):
+    top = stats[0][0:1, :]
+    for ref in stats[1:]:
+        top = jnp.maximum(top, ref[0:1, :])
+    total = jnp.zeros_like(top)
+    for ref in stats:
+        total = total + ref[1:2, :] * jnp.exp(ref[0:1, :] - top)
+    return top, total
+
+
+def join_kernel(first_ref, second_ref, out_ref):
+    top, total = joined((first_ref, second_ref))
+    row = lax.broadcasted_iota(jnp.int32, out_ref.shape, 0)
+    out_ref[...] = jnp.where(row == 0, top, total)
+
+
+def run_join(first, second):
+    return pl.pallas_call(
+        join_kernel,
+        out_shape=jax.ShapeDtypeStruct(first.shape, f32),
+        in_specs=[whole(), whole()],
+        out_specs=whole(),
+        compiler_params=pltpu.CompilerParams(vmem_limit_bytes=4 * MIB),
+        cost_estimate=pl.CostEstimate(flops=4096, bytes_accessed=4096, transcendentals=0),
+        name="pair_stats",
+    )(first, second)
+
+
+def turn_kernel(x_ref, gain_ref, out_ref):
+    out_ref[...] = (x_ref[...].astype(f32) * gain_ref[...]).T
+
+
+def run_turn(x, gain):
+    rows, features = x.shape
+    tile = 1024
+    return pl.pallas_call(
+        turn_kernel,
+        grid=(features // tile,),
+        out_shape=jax.ShapeDtypeStruct((features, rows), f32),
+        in_specs=[
+            pl.BlockSpec((rows, tile), lambda i: (0, i)),
+            pl.BlockSpec((1, tile), lambda i: (0, i)),
+        ],
+        out_specs=pl.BlockSpec((tile, rows), lambda i: (i, 0)),
+        compiler_params=pltpu.CompilerParams(vmem_limit_bytes=8 * MIB),
+        cost_estimate=pl.CostEstimate(flops=4096, bytes_accessed=4096, transcendentals=0),
+        name="turned_rows",
+    )(x, gain)
+
+
+def scale_kernel(
+    n_held, first, turned_ref, scale_ref, targets_ref, accepted_ref, weight_ref, *refs
+):
+    out_ref, target_ref = refs[n_held : n_held + 2]
+    rest_ref, sems = refs[-2:]
+    copies = column_copies(weight_ref, rest_ref, sems, first)
+    for copy in copies:
+        copy.start()
+    rows = turned_ref.shape[1]
+    scale = scale_ref[...].T[:1, :] * learn_rate
+    high, low = split2(turned_ref[...] * scale)
+    out_ref[:, :rows] = high
+    out_ref[:, rows:] = low
+    each = targets_ref.shape[1]
+    row = lax.broadcasted_iota(jnp.int32, (each, LANES), 0)
+    for block in range(rows // each):
+        target = jnp.zeros((each, LANES), jnp.int32)
+        for i in range(each):
+            target = jnp.where(row == i, targets_ref[block, i], target)
+        target = jnp.where(row < accepted_ref[block], target, -1)
+        target_ref[block * each : (block + 1) * each, :] = target
+    for copy in copies:
+        copy.wait()
+
+
+def run_scale(turned, scale, targets, accepted, weight, helds):
+    features, rows = turned.shape
+    first = sum(held.shape[1] for held in helds)
+    rest = weight.shape[1] - first
+    return pl.pallas_call(
+        functools.partial(scale_kernel, len(helds), first),
+        out_shape=(
+            jax.ShapeDtypeStruct((features, 2 * rows), bf16),
+            jax.ShapeDtypeStruct((rows, LANES), jnp.int32),
+        )
+        + held_shapes(helds)
+        + (pltpu.VMEM((features, rest), f32),),
+        in_specs=[
+            whole(),
+            whole(),
+            whole(pltpu.SMEM),
+            whole(pltpu.SMEM),
+            whole(pltpu.HBM),
+        ]
+        + [whole() for _ in helds],
+        out_specs=tuple(whole() for _ in range(3 + len(helds))),
+        input_output_aliases={5 + i: 2 + i for i in range(len(helds))},
+        scratch_shapes=[pltpu.SemaphoreType.DMA((rest // 256,))],
+        compiler_params=pltpu.CompilerParams(vmem_limit_bytes=8 * MIB),
+        cost_estimate=pl.CostEstimate(flops=65536, bytes_accessed=65536, transcendentals=0),
+        name="scaled_rows",
+    )(turned, scale, targets, accepted, in_hbm(weight), *helds)
+
+
+def update_kernel(n_tp, n_held, *refs):
+    turned_ref, target_ref = refs[:2]
+    expo_refs = refs[2 : 2 + n_tp]
+    n_stats = len(refs) - 2 - n_tp - 2 * n_held - 4
+    own_stat_ref, *stat_refs = refs[2 + n_tp : 2 + n_tp + n_stats]
+    out_ref, *held_refs = refs[2 + n_tp + n_stats + n_held : -3]
+    delta_buf, factor_buf, sems = refs[-3:]
+    rep, tp = lax.axis_index("rep"), lax.axis_index("tp")
+    share, columns = expo_refs[0].shape[0], expo_refs[0].shape[1] - LANES
+    rows = n_tp * share
+    top, total = joined(stat_refs)
+    factor = jnp.exp(own_stat_ref[0:1, :] - top) / total
+    factor = jnp.broadcast_to(factor, (rows, rows)).T
+    trained = jnp.where(target_ref[...] >= 0, 1.0, 0.0)
+    factor_buf[...] = factor[:, :LANES] * trained
+    label = lax.broadcasted_iota(jnp.int32, (share, columns), 1) + rep * columns
+    for k in range(n_tp):
+        place = pl.multiple_of(lax.bitwise_xor(tp, k) * share, share)
+        mine = pl.ds(place, share)
+        onehot = jnp.where(label == target_ref[mine, 0:1], 1.0, 0.0)
+        delta = expo_refs[k][:, :columns].astype(f32) * factor_buf[mine, 0:1] - onehot
+        delta = delta.astype(bf16)
+        delta_buf[mine, :] = delta
+        delta_buf[pl.ds(pl.multiple_of(rows + place, share), share), :] = delta
+
+    height = HEIGHT
+    steps = turned_ref.shape[0] // height
+
+    def copies_of(step):
+        mine = pl.ds(pl.multiple_of(step * height, height), height)
+        first, copies = 0, []
+        for index, ref in enumerate(held_refs):
+            target = out_ref.at[mine, pl.ds(first, ref.shape[1])]
+            copies.append(pltpu.make_async_copy(ref.at[mine], target, sems.at[index, step]))
+            first += ref.shape[1]
+        return copies
+
+    def one_step(step, _):
+        mine = pl.ds(pl.multiple_of(step * height, height), height)
+        grad = jnp.dot(turned_ref[mine, :], delta_buf[...], preferred_element_type=f32)
+        first = 0
+        for ref in held_refs:
+            ref[mine, :] = ref[mine, :] - grad[:, first : first + ref.shape[1]]
+            first += ref.shape[1]
+        for copy in copies_of(step):
+            copy.start()
+        return 0
+
+    def one_wait(step, _):
+        for copy in copies_of(step):
+            copy.wait()
+        return 0
+
+    lax.fori_loop(0, steps, one_step, 0)
+    lax.fori_loop(0, steps, one_wait, 0)
+
+
+def run_update(turned, target, expos, stats, helds):
+    features, pair = turned.shape
+    columns = sum(held.shape[1] for held in helds)
+    n_tp, n_held = len(expos), len(helds)
+    operands = (turned, target, *expos, *stats, *helds)
+    new_weight, *_ = pl.pallas_call(
+        functools.partial(update_kernel, n_tp, n_held),
+        out_shape=(jax.ShapeDtypeStruct((features, columns), f32),)
+        + held_shapes(helds),
+        in_specs=[whole() for _ in operands],
+        out_specs=(whole(pltpu.HBM),) + tuple(whole() for _ in helds),
+        input_output_aliases={len(operands) - n_held + i: 1 + i for i in range(n_held)},
+        scratch_shapes=[
+            pltpu.VMEM((pair, columns), bf16),
+            pltpu.VMEM((pair // 2, LANES), f32),
+            pltpu.SemaphoreType.DMA((n_held, features // HEIGHT)),
+        ],
+        compiler_params=pltpu.CompilerParams(vmem_limit_bytes=10 * MIB),
+        cost_estimate=pl.CostEstimate(flops=65536, bytes_accessed=65536, transcendentals=0),
+        name="weight_update",
+    )(*operands)
+    return new_weight
+
+
+def direct_plan(
+    queries,
+    cache_keys,
+    cache_values,
+    page_table,
+    lengths,
+    history,
+    norm_gain,
+    draft_weight,
+    targets,
+    accepted,
+):
+    n_rep, n_tp = lax.axis_size("rep"), lax.axis_size("tp")
+    gain = norm_gain.reshape(1, -1)
+    raw, attended, first = run_attention(
+        queries[0],
+        cache_keys[0, 0],
+        cache_values[0, 0],
+        page_table[0, 0],
+        lengths,
+        history[0],
+        draft_weight,
+        HELD[0],
     )
-    return (attended, draft_weight - learn_rate * grad)
+    first = pltpu.with_memory_space_constraint(first, pltpu.VMEM)
+    (second,), loaded = run_load(draft_weight, raw, HELD[0], HELD[1:])
+    raws = [raw] + [exchange(raw, "rep", k) for k in range(2, n_rep, 2)]
+    block = run_stack(raws, loaded)
+    blocks = (block, exchange(block, "rep", 1))
+    x, own, squares, *sends = run_logits(
+        blocks, gain, (first, second), draft_weight, n_rep, n_tp
+    )
+    turned = run_turn(x, gain)
+    received = [exchange(sends[k - 1], "tp", k) for k in range(1, n_tp)]
+    partly, part = run_first_sum(own, received[0])
+    helds, loaded = run_load(draft_weight, own, 0, AGAIN)
+    expo, scale, *helds = run_softmax(
+        partly, squares, part, received[1:], (loaded, turned), helds
+    )
+    expos = [expo] + [exchange(expo, "tp", k) for k in range(1, n_tp)]
+    scaled, target, *helds = run_scale(turned, scale, targets, accepted, draft_weight, helds)
+    stat, *helds = run_stats(expos, helds)
+    pair = run_join(stat, exchange(stat, "rep", 1))
+    stats = [stat, pair] + [exchange(pair, "rep", k) for k in range(2, n_rep, 2)]
+    helds = [pltpu.with_memory_space_constraint(held, pltpu.VMEM) for held in helds]
+    new_weight = run_update(scaled, target, expos, stats, helds)
+    return (attended[None], new_weight)
 
 
 def solution(mesh):
+    plan = direct_plan if (mesh.shape["rep"], mesh.shape["tp"]) == (8, 4) else general_plan
     return jax.shard_map(
-        on_device,
+        plan,
         mesh=mesh,
         in_specs=(
             P("rep", None, None),

time: 197 us -> 76.2 us (0.39)
  waiting for transfers between devices: 77.3 us -> 13.6 us
  matrix products: 61.6 us -> 0 us
  Pallas kernels: 0 us -> 43 us
  blocking collectives: 31 us -> 0 us
  starting transfers between devices: 0.08 us -> 17.4 us
  between operations: 14.9 us -> 1.42 us
  other arithmetic: 7.01 us -> 0 us
  local copies, waits for them, and re-layouts: 4.15 us -> 0.66 us
    dot_general x4 -> x0, matrix products: 61.6 us -> none  [the longest x1 35.1 us: on_device(): jnp.dot(gathered.T, delta, precision=lax.Precision.HIGHEST, preferred_ele...]
    psum x1 -> x0, waiting for transfers between devices: 51.1 us -> none  [on_device(): logits = lax.psum(partial_value, 'tp')]
    pallas_call x0 -> x12, Pallas kernels: none -> 43 us  [the longest x2 14.3 us: run_load(): pl.pallas_call(functools.partial(load_kernel, first, len(widths)), out_sh...]
    all_gather x1 -> x0, waiting for transfers between devices: 26.2 us -> none  [on_device(): gathered = lax.all_gather(scaled_rows, 'rep', axis=0, tiled=True)]
    all_gather x2 -> x0, blocking collectives: 17.6 us -> none  [merged(): pieces = jax.tree.map(lambda part: lax.all_gather(part, axis), value)]
    ppermute x0 -> x14, starting transfers between devices: none -> 17.4 us  [exchange(): return lax.ppermute(value, axis, pairs)]
    ppermute x0 -> x14, waiting for transfers between devices: none -> 13.6 us  [exchange(): return lax.ppermute(value, axis, pairs)]
    psum x1 -> x0, blocking collectives: 13.5 us -> none  [on_device(): squares = lax.psum(jnp.sum(wide * wide, axis=-1), 'tp')]
  transfers between devices with their start and end apart: 2 -> 14, of which waited for: 2 -> 7; matrix products, arithmetic and copies ran while one was open for 0% -> 0% of each run, Pallas kernels for 0% -> 26%
where the time goes in v1:
time: 76.2 us; the launch traced here: 76 us
  Pallas kernels  43 us (56%)
  starting transfers between devices  17.4 us (23%)
  waiting for transfers between devices  13.6 us (18%)
  between operations  1.42 us (2%)
    ppermute x14, starting transfers between devices, exchange(): return lax.ppermute(value, axis, pairs)  17.4 us
    pallas_call x2, Pallas kernels, run_load(): pl.pallas_call(functools.partial(load_kernel, first, len(widths)), out_sh...  14.3 us
    ppermute x14, waiting for transfers between devices, exchange(): return lax.ppermute(value, axis, pairs)  13.6 us
    pallas_call x1, Pallas kernels, run_update(): pl.pallas_call(functools.partial(update_kernel, n_tp, n_held), out_shape=...  11.9 us
    pallas_call x1, Pallas kernels, run_attention(): pl.pallas_call(functools.partial(attention_kernel, kv_local), out_shape=(...  6.18 us
    pallas_call x1, Pallas kernels, run_logits(): pl.pallas_call(functools.partial(logits_kernel, n_rep, n_tp), grid=(tiles...  4.77 us
    pallas_call x1, Pallas kernels, run_scale(): pl.pallas_call(functools.partial(scale_kernel, len(helds), first), out_sh...  4.1 us
  transfers between devices with their start and end apart: 14, of which 7 were waited for; matrix products, arithmetic and copies ran while one was open for 0% of the time, Pallas kernels for 26%

profile of v1, /device:TPU:0, one launch (start us, length us, event | category | flops | bytes accessed | tf_op | source)
XLA Modules:
  0.0 76.0 jit_solution(4615100030703959769)
XLA Ops:
  1.3 0.6 copy-done.2
  1.9 6.2 %attention.1 = (bf16[16,4096]{1,0:T(8,128)(2,1)S(1)}, bf16[4,4096]{1,0:T(4,128)(2,1)}, f32[4096,512]{1,0:T(8,128)S(1)}) custom-call(s32[16]{0:T(128)S(1)} %bitcast.9, s32[1]{0:T(128)S(6)} %copy.32.length_ref, bf16[4,16384]{1,0:T(4,128)(2,1)} %bitcast.12, bf16[16,64,256]{2,1,0:T(8,128)(2,1)} %bitcast.10, bf16[16,64,256]{2,1,0:T(8,128)(2,1)} %bitcast.11, ...), custom_call_target="tpu_custom_call" | custom-call | flops 67108864 | bytes 12582912 | tf_op jit(solution)/shard_map/attention/pallas_call | solution.py:247
  8.1 0.0 copy-start
  8.1 4.0 %collective-permute-start.2 = (bf16[16,4096]{1,0:T(8,128)(2,1)S(1)}, bf16[16,4096]{1,0:T(8,128)(2,1)S(1)}, u32[]{:S(2)}, u32[]{:S(2)}) collective-permute-start(bf16[16,4096]{1,0:T(8,128)(2,1)S(1)} %get-tuple-element.33.token_ref.refs_0_), channel_id=1, source_target_pairs={{0,24},{4,28},{8,16},{12,20},{16,8},{20,12},{24,0},{28,4},{1,25},{... | collective-permute-start | bytes 393224 | tf_op jit(solution)/shard_map/ppermute | solution.py:140
  12.1 0.5 collective-permute-start.1
  12.6 0.1 collective-permute-start
  12.7 5.9 %load_weight.2 = (f32[4096,1024]{1,0:T(8,128)S(1)}, f32[8,128]{1,0:T(8,128)S(1)}) custom-call(f32[4096,2048]{1,0:T(8,128)} %weight_ref.7, bf16[16,4096]{1,0:T(8,128)(2,1)S(1)} %get-tuple-element.33.token_ref.refs_0_), custom_call_target="tpu_custom_call" | custom-call | bytes 16777216 | tf_op jit(solution)/shard_map/load_weight/pallas_call | solution.py:311
  18.8 0.1 collective-permute-start.3
  18.8 1.9 %collective-permute-done.3.refs_1_ = bf16[64,4096]{1,0:T(8,128)(2,1)S(1)} collective-permute-done((bf16[64,4096]{1,0:T(8,128)(2,1)S(1)}, bf16[64,4096]{1,0:T(8,128)(2,1)S(1)}, u32[]{:S(2)}, u32[]{:S(2)}) %collective-permute-start.3) | collective-permute-done | bytes 524320 | tf_op jit(solution)/shard_map/ppermute | solution.py:140
  20.7 4.8 %partial_logits.1 = (bf16[128,4096]{1,0:T(8,128)(2,1)S(1)}, f32[32,2048]{1,0:T(8,128)S(1)}, f32[128,128]{1,0:T(8,128)S(1)}, s16[32,2176]{1,0:T(8,128)(2,1)S(1)},...) custom-call(bf16[64,4096]{1,0:T(8,128)(2,1)S(1)} %stacked_rows.1.refs_0_, ...), custom_call_target="tpu_custom_call" | custom-call | flops 6442450944 | bytes 33554432 | tf_op jit(solution)/shard_map/partial_logits/pallas_call | solution.py:441
  25.5 2.0 %collective-permute-start.4 = (s16[32,2176]{1,0:T(8,128)(2,1)S(1)}, s16[32,2176]{1,0:T(8,128)(2,1)S(1)}, u32[]{:S(2)}, u32[]{:S(2)}) collective-permute-start(s16[32,2176]{1,0:T(8,128)(2,1)S(1)} %get-tuple-element.39), channel_id=1, source_target_pairs={{0,1},{1,0},{2,3},{3,2},{4,5},{5,4},{6,7},{7,6},{8,9},{9,8},{10,11... | collective-permute-start | bytes 417800 | tf_op jit(solution)/shard_map/ppermute | solution.py:140
  27.5 2.6 %collective-permute-start.5 = (s16[32,2176]{1,0:T(8,128)(2,1)S(1)}, s16[32,2176]{1,0:T(8,128)(2,1)S(1)}, u32[]{:S(2)}, u32[]{:S(2)}) collective-permute-start(s16[32,2176]{1,0:T(8,128)(2,1)S(1)} %get-tuple-element.43), channel_id=1, source_target_pairs={{0,2},{1,3},{2,0},{3,1},{4,6},{5,7},{6,4},{7,5},{8,10},{9,11},{10,... | collective-permute-start | bytes 417800 | tf_op jit(solution)/shard_map/ppermute | solution.py:140
  30.1 0.9 %turned_rows.1.refs_3_.turned_ref = f32[4096,128]{1,0:T(8,128)S(1)} custom-call(bf16[128,4096]{1,0:T(8,128)(2,1)S(1)} %get-tuple-element.37.x_ref, f32[1,4096]{1,0:T(1,128)S(1)} %bitcast.8), custom_call_target="tpu_custom_call" | custom-call | flops 4096 | bytes 4096 | tf_op jit(solution)/shard_map/turned_rows/pallas_call | solution.py:619
  31.1 8.4 %load_weight.3 = (f32[4096,1024]{1,0:T(8,128)S(1)}, f32[4096,512]{1,0:T(8,128)S(1)}, f32[8,128]{1,0:T(8,128)S(1)}) custom-call(f32[4096,2048]{1,0:T(8,128)} %weight_ref.7, f32[32,2048]{1,0:T(8,128)S(1)} %get-tuple-element.38.own_ref.token_ref), custom_call_target="tpu_custom_call" | custom-call | bytes 25165824 | tf_op jit(solution)/shard_map/load_weight/pallas_call | solution.py:311
  39.5 0.1 first_sum.1
  39.6 1.4 %collective-permute-done.5.refs_0_ = s16[32,2176]{1,0:T(8,128)(2,1)S(1)} collective-permute-done((s16[32,2176]{1,0:T(8,128)(2,1)S(1)}, s16[32,2176]{1,0:T(8,128)(2,1)S(1)}, u32[]{:S(2)}, u32[]{:S(2)}) %collective-permute-start.5) | collective-permute-done | bytes 139296 | tf_op jit(solution)/shard_map/ppermute | solution.py:140
  41.0 0.4 local_softmax.1
  41.4 2.5 %collective-permute-start.9 = (bf16[32,2176]{1,0:T(8,128)(2,1)S(1)}, bf16[32,2176]{1,0:T(8,128)(2,1)S(1)}, u32[]{:S(2)}, u32[]{:S(2)}) collective-permute-start(bf16[32,2176]{1,0:T(8,128)(2,1)S(1)} %get-tuple-element.53.refs_0_.refs_2_), channel_id=1, source_target_pairs={{0,3},{1,2},{2,1},{3,0},{4,7},{5,6},{6,5},{7,4},{8,11},{9,10},{10,... | collective-permute-start | bytes 417800 | tf_op jit(solution)/shard_map/ppermute | solution.py:140
  43.9 1.5 %collective-permute-start.8 = (bf16[32,2176]{1,0:T(8,128)(2,1)S(1)}, bf16[32,2176]{1,0:T(8,128)(2,1)S(1)}, u32[]{:S(2)}, u32[]{:S(2)}) collective-permute-start(bf16[32,2176]{1,0:T(8,128)(2,1)S(1)} %get-tuple-element.53.refs_0_.refs_2_), channel_id=1, source_target_pairs={{0,2},{1,3},{2,0},{3,1},{4,6},{5,7},{6,4},{7,5},{8,10},{9,11},{10,... | collective-permute-start | bytes 417800 | tf_op jit(solution)/shard_map/ppermute | solution.py:140
  45.4 0.5 collective-permute-start.7
  45.8 4.1 %scaled_rows.1 = (bf16[4096,256]{1,0:T(8,128)(2,1)S(1)}, s32[128,128]{1,0:T(8,128)S(1)}, f32[4096,1024]{1,0:T(8,128)S(1)}, f32[4096,512]{1,0:T(8,128)S(1)}, f32[4096,512]{1,0:T(8,128)S(1)}) custom-call(f32[4096,128]{1,0:T(8,128)S(1)} %turned_rows.1.refs_3_.turned_ref, ...), custom_call_target="tpu_custom_call", output_to_operand_aliasing={{2}: (5, {}), {3}: (6, {})} | custom-call | flops 65536 | bytes 65536 | tf_op jit(solution)/shard_map/scaled_rows/pallas_call | solution.py:663
  50.0 6.0 %collective-permute-done.8.refs_2_.refs_4_ = bf16[32,2176]{1,0:T(8,128)(2,1)S(1)} collective-permute-done((bf16[32,2176]{1,0:T(8,128)(2,1)S(1)}, bf16[32,2176]{1,0:T(8,128)(2,1)S(1)}, u32[]{:S(2)}, u32[]{:S(2)}) %collective-permute-start.8) | collective-permute-done | bytes 139296 | tf_op jit(solution)/shard_map/ppermute | solution.py:140
  56.0 0.2 row_stats.1
  56.2 0.0 collective-permute-start.10
  56.3 1.2 %collective-permute-done.10.second_ref = f32[8,128]{1,0:T(8,128)S(1)} collective-permute-done((f32[8,128]{1,0:T(8,128)S(1)}, f32[8,128]{1,0:T(8,128)S(1)}, u32[]{:S(2)}, u32[]{:S(2)}) %collective-permute-start.10) | collective-permute-done | bytes 4128 | tf_op jit(solution)/shard_map/ppermute | solution.py:140
  57.4 2.5 %collective-permute-start.13 = (f32[8,128]{1,0:T(8,128)S(1)}, f32[8,128]{1,0:T(8,128)S(1)}, u32[]{:S(2)}, u32[]{:S(2)}) collective-permute-start(f32[8,128]{1,0:T(8,128)S(1)} %pair_stats.1.refs_7_), channel_id=1, source_target_pairs={{0,24},{4,28},{8,16},{12,20},{16,8},{20,12},{24,0},{28,4},{1,25},{... | collective-permute-start | bytes 12296 | tf_op jit(solution)/shard_map/ppermute | solution.py:140
  60.0 0.5 collective-permute-start.12
  60.5 0.5 collective-permute-start.11
  61.0 1.0 %collective-permute-done.13.refs_10_ = f32[8,128]{1,0:T(8,128)S(1)} collective-permute-done((f32[8,128]{1,0:T(8,128)S(1)}, f32[8,128]{1,0:T(8,128)S(1)}, u32[]{:S(2)}, u32[]{:S(2)}) %collective-permute-start.13) | collective-permute-done | bytes 4128 | tf_op jit(solution)/shard_map/ppermute | solution.py:140
  62.0 1.5 %collective-permute-done.12.refs_9_ = f32[8,128]{1,0:T(8,128)S(1)} collective-permute-done((f32[8,128]{1,0:T(8,128)S(1)}, f32[8,128]{1,0:T(8,128)S(1)}, u32[]{:S(2)}, u32[]{:S(2)}) %collective-permute-start.12) | collective-permute-done | bytes 4128 | tf_op jit(solution)/shard_map/ppermute | solution.py:140
  63.6 0.5 collective-permute-done.11.refs_8_
  64.1 11.9 %weight_update.1 = (f32[4096,2048]{1,0:T(8,128)}, f32[4096,1024]{1,0:T(8,128)S(1)}, f32[4096,512]{1,0:T(8,128)S(1)}, f32[4096,512]{1,0:T(8,128)S(1)}) custom-call(bf16[4096,256]{1,0:T(8,128)(2,1)S(1)} %get-tuple-element.51.refs_0_, s32[128,128]{1,0:T(8,128)S(1)} %get-tuple-element.52.refs_1_, ...), custom_call_target="tpu_custom_call", output_to_operand_aliasing={{1}: (11, {}), {2}: (12, {}), {3}: (13, {})} | custom-call | flops 65536 | bytes 65536 | tf_op jit(solution)/shard_map/weight_update/pallas_call | solution.py:750
  (16 shorter events, 0.1 us)
Async XLA Ops:
  1.3 0.7 copy-start.2
  8.1 12.6 %copy-start = (f32[4096]{0:T(1024)S(1)}, f32[4096]{0:T(1024)}, u32[]{:S(2)}) copy-start(f32[4096]{0:T(1024)} %param.16) | copy-start | bytes 49156
  8.1 10.5 %collective-permute-start.2 = (bf16[16,4096]{1,0:T(8,128)(2,1)S(1)}, bf16[16,4096]{1,0:T(8,128)(2,1)S(1)}, u32[]{:S(2)}, u32[]{:S(2)}) collective-permute-start(bf16[16,4096]{1,0:T(8,128)(2,1)S(1)} %get-tuple-element.33.token_ref.refs_0_), channel_id=1, source_target_pairs={{0,24},{4,28},{8,16},{12,20},{16,8},{20,12},{24,0},{28,4},{1,25},{... | collective-permute-start | bytes 393224 | tf_op jit(solution)/shard_map/ppermute | solution.py:140
  12.1 6.6 %collective-permute-start.1 = (bf16[16,4096]{1,0:T(8,128)(2,1)S(1)}, bf16[16,4096]{1,0:T(8,128)(2,1)S(1)}, u32[]{:S(2)}, u32[]{:S(2)}) collective-permute-start(bf16[16,4096]{1,0:T(8,128)(2,1)S(1)} %get-tuple-element.33.token_ref.refs_0_), channel_id=1, source_target_pairs={{0,16},{4,20},{8,24},{12,28},{16,0},{20,4},{24,8},{28,12},{1,17},{... | collective-permute-start | bytes 393224 | tf_op jit(solution)/shard_map/ppermute | solution.py:140
  12.6 6.1 %collective-permute-start = (bf16[16,4096]{1,0:T(8,128)(2,1)S(1)}, bf16[16,4096]{1,0:T(8,128)(2,1)S(1)}, u32[]{:S(2)}, u32[]{:S(2)}) collective-permute-start(bf16[16,4096]{1,0:T(8,128)(2,1)S(1)} %get-tuple-element.33.token_ref.refs_0_), channel_id=1, source_target_pairs={{0,8},{4,12},{8,0},{12,4},{16,24},{20,28},{24,16},{28,20},{1,9},{5... | collective-permute-start | bytes 393224 | tf_op jit(solution)/shard_map/ppermute | solution.py:140
  18.8 2.0 %collective-permute-start.3 = (bf16[64,4096]{1,0:T(8,128)(2,1)S(1)}, bf16[64,4096]{1,0:T(8,128)(2,1)S(1)}, u32[]{:S(2)}, u32[]{:S(2)}) collective-permute-start(bf16[64,4096]{1,0:T(8,128)(2,1)S(1)} %stacked_rows.1.refs_0_), channel_id=1, source_target_pairs={{0,4},{4,0},{8,12},{12,8},{16,20},{20,16},{24,28},{28,24},{1,5},{5... | collective-permute-start | bytes 1572872 | tf_op jit(solution)/shard_map/ppermute | solution.py:140
  25.5 14.0 %collective-permute-start.4 = (s16[32,2176]{1,0:T(8,128)(2,1)S(1)}, s16[32,2176]{1,0:T(8,128)(2,1)S(1)}, u32[]{:S(2)}, u32[]{:S(2)}) collective-permute-start(s16[32,2176]{1,0:T(8,128)(2,1)S(1)} %get-tuple-element.39), channel_id=1, source_target_pairs={{0,1},{1,0},{2,3},{3,2},{4,5},{5,4},{6,7},{7,6},{8,9},{9,8},{10,11... | collective-permute-start | bytes 417800 | tf_op jit(solution)/shard_map/ppermute | solution.py:140
  27.5 13.4 %collective-permute-start.5 = (s16[32,2176]{1,0:T(8,128)(2,1)S(1)}, s16[32,2176]{1,0:T(8,128)(2,1)S(1)}, u32[]{:S(2)}, u32[]{:S(2)}) collective-permute-start(s16[32,2176]{1,0:T(8,128)(2,1)S(1)} %get-tuple-element.43), channel_id=1, source_target_pairs={{0,2},{1,3},{2,0},{3,1},{4,6},{5,7},{6,4},{7,5},{8,10},{9,11},{10,... | collective-permute-start | bytes 417800 | tf_op jit(solution)/shard_map/ppermute | solution.py:140
  30.1 10.8 %collective-permute-start.6 = (s16[32,2176]{1,0:T(8,128)(2,1)S(1)}, s16[32,2176]{1,0:T(8,128)(2,1)S(1)}, u32[]{:S(2)}, u32[]{:S(2)}) collective-permute-start(s16[32,2176]{1,0:T(8,128)(2,1)S(1)} %get-tuple-element.44), channel_id=1, source_target_pairs={{0,3},{1,2},{2,1},{3,0},{4,7},{5,6},{6,5},{7,4},{8,11},{9,10},{10,... | collective-permute-start | bytes 417800 | tf_op jit(solution)/shard_map/ppermute | solution.py:140
  41.0 4.9 %copy-start.1 = (s32[8,16]{1,0:T(8,128)S(1)}, s32[8,16]{1,0:T(8,128)}, u32[]{:S(2)}) copy-start(s32[8,16]{1,0:T(8,128)} %targets_ref.1) | copy-start | bytes 1540
  41.0 4.9 %copy-start.3 = (s32[8]{0:T(128)S(1)}, s32[8]{0:T(128)}, u32[]{:S(2)}) copy-start(s32[8]{0:T(128)} %accepted_ref.1) | copy-start | bytes 100
  41.4 8.6 %collective-permute-start.9 = (bf16[32,2176]{1,0:T(8,128)(2,1)S(1)}, bf16[32,2176]{1,0:T(8,128)(2,1)S(1)}, u32[]{:S(2)}, u32[]{:S(2)}) collective-permute-start(bf16[32,2176]{1,0:T(8,128)(2,1)S(1)} %get-tuple-element.53.refs_0_.refs_2_), channel_id=1, source_target_pairs={{0,3},{1,2},{2,1},{3,0},{4,7},{5,6},{6,5},{7,4},{8,11},{9,10},{10,... | collective-permute-start | bytes 417800 | tf_op jit(solution)/shard_map/ppermute | solution.py:140
  43.9 12.1 %collective-permute-start.8 = (bf16[32,2176]{1,0:T(8,128)(2,1)S(1)}, bf16[32,2176]{1,0:T(8,128)(2,1)S(1)}, u32[]{:S(2)}, u32[]{:S(2)}) collective-permute-start(bf16[32,2176]{1,0:T(8,128)(2,1)S(1)} %get-tuple-element.53.refs_0_.refs_2_), channel_id=1, source_target_pairs={{0,2},{1,3},{2,0},{3,1},{4,6},{5,7},{6,4},{7,5},{8,10},{9,11},{10,... | collective-permute-start | bytes 417800 | tf_op jit(solution)/shard_map/ppermute | solution.py:140
  45.4 10.6 %collective-permute-start.7 = (bf16[32,2176]{1,0:T(8,128)(2,1)S(1)}, bf16[32,2176]{1,0:T(8,128)(2,1)S(1)}, u32[]{:S(2)}, u32[]{:S(2)}) collective-permute-start(bf16[32,2176]{1,0:T(8,128)(2,1)S(1)} %get-tuple-element.53.refs_0_.refs_2_), channel_id=1, source_target_pairs={{0,1},{1,0},{2,3},{3,2},{4,5},{5,4},{6,7},{7,6},{8,9},{9,8},{10,11... | collective-permute-start | bytes 417800 | tf_op jit(solution)/shard_map/ppermute | solution.py:140
  56.2 1.2 %collective-permute-start.10 = (f32[8,128]{1,0:T(8,128)S(1)}, f32[8,128]{1,0:T(8,128)S(1)}, u32[]{:S(2)}, u32[]{:S(2)}) collective-permute-start(f32[8,128]{1,0:T(8,128)S(1)} %get-tuple-element.57.first_ref.refs_6_), channel_id=1, source_target_pairs={{0,4},{4,0},{8,12},{12,8},{16,20},{20,16},{24,28},{28,24},{1,5},{5... | collective-permute-start | bytes 12296 | tf_op jit(solution)/shard_map/ppermute | solution.py:140
  57.4 4.6 %collective-permute-start.13 = (f32[8,128]{1,0:T(8,128)S(1)}, f32[8,128]{1,0:T(8,128)S(1)}, u32[]{:S(2)}, u32[]{:S(2)}) collective-permute-start(f32[8,128]{1,0:T(8,128)S(1)} %pair_stats.1.refs_7_), channel_id=1, source_target_pairs={{0,24},{4,28},{8,16},{12,20},{16,8},{20,12},{24,0},{28,4},{1,25},{... | collective-permute-start | bytes 12296 | tf_op jit(solution)/shard_map/ppermute | solution.py:140
  60.0 3.6 %collective-permute-start.12 = (f32[8,128]{1,0:T(8,128)S(1)}, f32[8,128]{1,0:T(8,128)S(1)}, u32[]{:S(2)}, u32[]{:S(2)}) collective-permute-start(f32[8,128]{1,0:T(8,128)S(1)} %pair_stats.1.refs_7_), channel_id=1, source_target_pairs={{0,16},{4,20},{8,24},{12,28},{16,0},{20,4},{24,8},{28,12},{1,17},{... | collective-permute-start | bytes 12296 | tf_op jit(solution)/shard_map/ppermute | solution.py:140
  60.5 3.6 %collective-permute-start.11 = (f32[8,128]{1,0:T(8,128)S(1)}, f32[8,128]{1,0:T(8,128)S(1)}, u32[]{:S(2)}, u32[]{:S(2)}) collective-permute-start(f32[8,128]{1,0:T(8,128)S(1)} %pair_stats.1.refs_7_), channel_id=1, source_target_pairs={{0,8},{4,12},{8,0},{12,4},{16,24},{20,28},{24,16},{28,20},{1,9},{5... | collective-permute-start | bytes 12296 | tf_op jit(solution)/shard_map/ppermute | solution.py:140

commit v2 on v1

--- a/solution.py
+++ b/solution.py
@@ -16,9 +16,11 @@
 LANES = 128
 MIB = 1024 * 1024
 TILE = 512
+SUM_ORDER = (2, 1, 3)
+BACK_ORDER = (1, 2, 3)
 HEIGHT = 256
 HELD = (512, 1024)
-AGAIN = (1024, 512)
+AGAIN = (768, 1024)
 bf16 = jnp.bfloat16
 f32 = jnp.float32
 
@@ -477,35 +479,13 @@
     return value * jnp.exp2(tail[:, 3:4] - 15.0), tail * unit
 
 
-def first_sum_kernel(own_ref, received_ref, sum_ref, square_ref):
-    value, squares = decoded(received_ref, own_ref.shape[1])
-    sum_ref[...] = own_ref[...] + value
-    square_ref[...] = squares
-
-
-def run_first_sum(own, received):
-    share, columns = own.shape
-    return pl.pallas_call(
-        first_sum_kernel,
-        out_shape=(
-            jax.ShapeDtypeStruct((share, columns), f32),
-            jax.ShapeDtypeStruct((share, LANES), f32),
-        ),
-        in_specs=[whole(), whole()],
-        out_specs=(whole(), whole()),
-        compiler_params=pltpu.CompilerParams(vmem_limit_bytes=8 * MIB),
-        cost_estimate=pl.CostEstimate(flops=65536, bytes_accessed=65536, transcendentals=0),
-        name="first_sum",
-    )(own, received)
-
-
-def softmax_kernel(n_tp, n_more, sum_ref, square_ref, first_ref, *refs):
-    received = refs[: n_tp - 2]
-    expo_ref, scale_ref = refs[n_tp - 2 + n_more : n_tp + n_more]
-    share, columns = sum_ref.shape
+def softmax_kernel(n_tp, n_more, own_ref, square_ref, *refs):
+    received = refs[: n_tp - 1]
+    left_ref, right_ref, scale_ref = refs[n_tp - 1 + n_more : n_tp + 2 + n_more]
+    share, columns = own_ref.shape
     group = LANES // n_tp
     lane = lax.broadcasted_iota(jnp.int32, (share, LANES), 1)
-    logits, squares = sum_ref[...], first_ref[...]
+    logits, squares = own_ref[...], jnp.zeros((share, LANES), f32)
     for ref in received:
         value, more = decoded(ref, columns)
         logits, squares = logits + value, squares + more
@@ -520,36 +500,41 @@
     top = jnp.max(logits, axis=-1, keepdims=True)
     expo = jnp.exp(logits - top)
     total = jnp.sum(expo, axis=-1, keepdims=True)
-    expo_ref[:, :columns] = expo.astype(bf16)
-    for first, value in ((0, top), (3, total)):
-        for place in range(first, first + 3):
+    width = right_ref.shape[1]
+    place = columns - width
+    left_ref[:, :place] = expo[:, :place].astype(bf16)
+    right_ref[...] = expo[:, place:].astype(bf16)
+    for value in (top, total):
+        for _ in range(3):
             high = value.astype(bf16)
-            expo_ref[:, columns + place : columns + place + 1] = high
+            left_ref[:, place : place + 1] = high
             value = value - high.astype(f32)
+            place += 1
 
 
 def held_shapes(helds):
     return tuple(pltpu.VMEM(held.shape, f32) for held in helds)
 
 
-def run_softmax(partly, squares, first, received, after, helds):
-    share, columns = partly.shape
+def run_softmax(own, squares, received, after, helds):
+    share, columns = own.shape
     rows = squares.shape[0]
     return pl.pallas_call(
-        functools.partial(softmax_kernel, len(received) + 2, len(after) + len(helds)),
+        functools.partial(softmax_kernel, len(received) + 1, len(after) + len(helds)),
         out_shape=(
-            jax.ShapeDtypeStruct((share, columns + LANES), bf16),
+            jax.ShapeDtypeStruct((share, AGAIN[0] + LANES), bf16),
+            jax.ShapeDtypeStruct((share, columns - AGAIN[0]), bf16),
             jax.ShapeDtypeStruct((rows, LANES), f32),
         )
         + held_shapes(helds),
-        in_specs=[whole() for _ in range(len(received) + 3)] + [whole(pl.ANY) for _ in after]
+        in_specs=[whole() for _ in range(len(received) + 2)] + [whole(pl.ANY) for _ in after]
         + [whole() for _ in helds],
-        out_specs=tuple(whole() for _ in range(2 + len(helds))),
-        input_output_aliases={len(received) + len(after) + 3 + i: 2 + i for i in range(len(helds))},
+        out_specs=tuple(whole() for _ in range(3 + len(helds))),
+        input_output_aliases={len(received) + len(after) + 2 + i: 3 + i for i in range(len(helds))},
         compiler_params=pltpu.CompilerParams(vmem_limit_bytes=8 * MIB),
         cost_estimate=pl.CostEstimate(flops=65536, bytes_accessed=65536, transcendentals=0),
         name="local_softmax",
-    )(partly, squares, first, *received, *after, *helds)
+    )(own, squares, *received, *after, *helds)
 
 
 def stats_kernel(n_tp, n_held, *refs):
@@ -557,7 +542,7 @@
     share = stats[0].shape[0]
     tp = lax.axis_index("tp")
     lane = lax.broadcasted_iota(jnp.int32, (share, LANES), 1)
-    for k, ref in enumerate(stats):
+    for k, ref in zip((0, *BACK_ORDER), stats):
         parts = ref[:, ref.shape[1] - LANES :].astype(f32)
         top = parts[:, 0:1] + parts[:, 1:2] + parts[:, 2:3]
         total = parts[:, 3:4] + parts[:, 4:5] + parts[:, 5:6]
@@ -685,27 +670,26 @@
     )(turned, scale, targets, accepted, in_hbm(weight), *helds)
 
 
-def update_kernel(n_tp, n_held, *refs):
+def update_kernel(n_tp, n_held, n_kept, first, total_columns, *refs):
     turned_ref, target_ref = refs[:2]
     expo_refs = refs[2 : 2 + n_tp]
-    n_stats = len(refs) - 2 - n_tp - 2 * n_held - 4
-    own_stat_ref, *stat_refs = refs[2 + n_tp : 2 + n_tp + n_stats]
-    out_ref, *held_refs = refs[2 + n_tp + n_stats + n_held : -3]
+    own_stat_ref, *stat_refs = refs[2 + n_tp : 3 + 2 * n_tp]
+    out_ref, *held_refs = refs[-4 - n_held - n_kept : -3 - n_kept]
     delta_buf, factor_buf, sems = refs[-3:]
     rep, tp = lax.axis_index("rep"), lax.axis_index("tp")
-    share, columns = expo_refs[0].shape[0], expo_refs[0].shape[1] - LANES
-    rows = n_tp * share
+    share = expo_refs[0].shape[0]
+    rows, columns = n_tp * share, delta_buf.shape[1]
     top, total = joined(stat_refs)
     factor = jnp.exp(own_stat_ref[0:1, :] - top) / total
     factor = jnp.broadcast_to(factor, (rows, rows)).T
     trained = jnp.where(target_ref[...] >= 0, 1.0, 0.0)
     factor_buf[...] = factor[:, :LANES] * trained
-    label = lax.broadcasted_iota(jnp.int32, (share, columns), 1) + rep * columns
-    for k in range(n_tp):
+    label = lax.broadcasted_iota(jnp.int32, (share, columns), 1) + (rep * total_columns + first)
+    for k, ref in zip((0, *BACK_ORDER), expo_refs):
         place = pl.multiple_of(lax.bitwise_xor(tp, k) * share, share)
         mine = pl.ds(place, share)
         onehot = jnp.where(label == target_ref[mine, 0:1], 1.0, 0.0)
-        delta = expo_refs[k][:, :columns].astype(f32) * factor_buf[mine, 0:1] - onehot
+        delta = ref[:, :columns].astype(f32) * factor_buf[mine, 0:1] - onehot
         delta = delta.astype(bf16)
         delta_buf[mine, :] = delta
         delta_buf[pl.ds(pl.multiple_of(rows + place, share), share), :] = delta
@@ -715,20 +699,20 @@
 
     def copies_of(step):
         mine = pl.ds(pl.multiple_of(step * height, height), height)
-        first, copies = 0, []
+        place, copies = first, []
         for index, ref in enumerate(held_refs):
-            target = out_ref.at[mine, pl.ds(first, ref.shape[1])]
+            target = out_ref.at[mine, pl.ds(place, ref.shape[1])]
             copies.append(pltpu.make_async_copy(ref.at[mine], target, sems.at[index, step]))
-            first += ref.shape[1]
+            place += ref.shape[1]
         return copies
 
     def one_step(step, _):
         mine = pl.ds(pl.multiple_of(step * height, height), height)
         grad = jnp.dot(turned_ref[mine, :], delta_buf[...], preferred_element_type=f32)
-        first = 0
+        place = 0
         for ref in held_refs:
-            ref[mine, :] = ref[mine, :] - grad[:, first : first + ref.shape[1]]
-            first += ref.shape[1]
+            ref[mine, :] = ref[mine, :] - grad[:, place : place + ref.shape[1]]
+            place += ref.shape[1]
         for copy in copies_of(step):
             copy.start()
         return 0
@@ -742,28 +726,39 @@
     lax.fori_loop(0, steps, one_wait, 0)
 
 
-def run_update(turned, target, expos, stats, helds):
+def run_update(turned, target, expos, stats, helds, kept, first, total_columns, out=None):
     features, pair = turned.shape
     columns = sum(held.shape[1] for held in helds)
     n_tp, n_held = len(expos), len(helds)
-    operands = (turned, target, *expos, *stats, *helds)
-    new_weight, *_ = pl.pallas_call(
-        functools.partial(update_kernel, n_tp, n_held),
-        out_shape=(jax.ShapeDtypeStruct((features, columns), f32),)
-        + held_shapes(helds),
-        in_specs=[whole() for _ in operands],
-        out_specs=(whole(pltpu.HBM),) + tuple(whole() for _ in helds),
-        input_output_aliases={len(operands) - n_held + i: 1 + i for i in range(n_held)},
+    earlier = () if out is None else (out,)
+    pieces = (*helds, *kept)
+    inputs = (turned, target, *expos, *stats)
+    before = len(inputs) + len(earlier)
+    aliases = {before + i: 1 + i for i in range(len(pieces))}
+    if earlier:
+        aliases[len(inputs)] = 0
+    new_weight, *pieces = pl.pallas_call(
+        functools.partial(update_kernel, n_tp, n_held, len(kept), first, total_columns),
+        out_shape=(jax.ShapeDtypeStruct((features, total_columns), f32),) + held_shapes(pieces),
+        in_specs=[whole() for _ in inputs]
+        + [whole(pltpu.HBM) for _ in earlier]
+        + [whole() for _ in pieces],
+        out_specs=(whole(pltpu.HBM),) + tuple(whole() for _ in pieces),
+        input_output_aliases=aliases,
         scratch_shapes=[
             pltpu.VMEM((pair, columns), bf16),
             pltpu.VMEM((pair // 2, LANES), f32),
             pltpu.SemaphoreType.DMA((n_held, features // HEIGHT)),
         ],
         compiler_params=pltpu.CompilerParams(vmem_limit_bytes=10 * MIB),
-        cost_estimate=pl.CostEstimate(flops=65536, bytes_accessed=65536, transcendentals=0),
+        cost_estimate=pl.CostEstimate(
+            flops=2 * pair * features * columns,
+            bytes_accessed=4 * features * columns,
+            transcendentals=0,
+        ),
         name="weight_update",
-    )(*operands)
-    return new_weight
+    )(*inputs, *earlier, *pieces)
+    return new_weight, pieces[n_held:]
 
 
 def direct_plan(
@@ -799,19 +794,24 @@
         blocks, gain, (first, second), draft_weight, n_rep, n_tp
     )
     turned = run_turn(x, gain)
-    received = [exchange(sends[k - 1], "tp", k) for k in range(1, n_tp)]
-    partly, part = run_first_sum(own, received[0])
+    received = [exchange(sends[k - 1], "tp", k) for k in SUM_ORDER]
     helds, loaded = run_load(draft_weight, own, 0, AGAIN)
-    expo, scale, *helds = run_softmax(
-        partly, squares, part, received[1:], (loaded, turned), helds
-    )
-    expos = [expo] + [exchange(expo, "tp", k) for k in range(1, n_tp)]
+    left, right, scale, *helds = run_softmax(own, squares, received, (loaded, turned), helds)
+    lefts = [left] + [exchange(left, "tp", k) for k in BACK_ORDER]
     scaled, target, *helds = run_scale(turned, scale, targets, accepted, draft_weight, helds)
-    stat, *helds = run_stats(expos, helds)
+    stat, *helds = run_stats(lefts, helds)
     pair = run_join(stat, exchange(stat, "rep", 1))
     stats = [stat, pair] + [exchange(pair, "rep", k) for k in range(2, n_rep, 2)]
     helds = [pltpu.with_memory_space_constraint(held, pltpu.VMEM) for held in helds]
-    new_weight = run_update(scaled, target, expos, stats, helds)
+    columns = draft_weight.shape[1]
+    new_weight, kept = run_update(
+        scaled, target, lefts, stats, helds[:1], helds[1:], 0, columns
+    )
+    kept = [pltpu.with_memory_space_constraint(held, pltpu.VMEM) for held in kept]
+    rights = [right] + [exchange(right, "tp", k) for k in BACK_ORDER]
+    new_weight, _ = run_update(
+        scaled, target, rights, stats, kept, (), AGAIN[0], columns, new_weight
+    )
     return (attended[None], new_weight)
 
 

time: 76.2 us -> 73.8 us (0.969)
  waiting for transfers between devices: 13.6 us -> 5.1 us
  starting transfers between devices: 17.4 us -> 21.8 us
  Pallas kernels: 43 us -> 44.5 us
    ppermute x14 -> x17, waiting for transfers between devices: 13.6 us -> 5.1 us  [exchange(): return lax.ppermute(value, axis, pairs)]
    ppermute x14 -> x17, starting transfers between devices: 17.4 us -> 21.8 us  [exchange(): return lax.ppermute(value, axis, pairs)]
    pallas_call x3, Pallas kernels: 12.4 us -> 14 us  [the longest x2 13.6 us: run_update(): pl.pallas_call(functools.partial(update_kernel, n_tp, n_held, len(kept),...]
    pallas_call x1, Pallas kernels: 4.1 us -> 2.8 us  [run_scale(): pl.pallas_call(functools.partial(scale_kernel, len(helds), first), out_sh...]
    pallas_call x2, Pallas kernels: 14.3 us -> 15.5 us  [run_load(): pl.pallas_call(functools.partial(load_kernel, first, len(widths)), out_sh...]
  transfers between devices with their start and end apart: 14 -> 17, of which waited for: 7 -> 3; matrix products, arithmetic and copies ran while one was open for 0% -> 0% of each run, Pallas kernels for 26% -> 34%
where the time goes in v2:
time: 73.8 us; the launch traced here: 73.5 us
  Pallas kernels  44.5 us (60%)
  starting transfers between devices  21.8 us (30%)
  waiting for transfers between devices  5.1 us (7%)
  between operations  1.48 us (2%)
    ppermute x17, starting transfers between devices, exchange(): return lax.ppermute(value, axis, pairs)  21.8 us
    pallas_call x2, Pallas kernels, run_load(): pl.pallas_call(functools.partial(load_kernel, first, len(widths)), out_sh...  15.5 us
    pallas_call x2, Pallas kernels, run_update(): pl.pallas_call(functools.partial(update_kernel, n_tp, n_held, len(kept),...  13.6 us
    pallas_call x1, Pallas kernels, run_attention(): pl.pallas_call(functools.partial(attention_kernel, kv_local), out_shape=(...  6.18 us
    ppermute x17, waiting for transfers between devices, exchange(): return lax.ppermute(value, axis, pairs)  5.1 us
    pallas_call x1, Pallas kernels, run_logits(): pl.pallas_call(functools.partial(logits_kernel, n_rep, n_tp), grid=(tiles...  4.77 us
    pallas_call x1, Pallas kernels, run_scale(): pl.pallas_call(functools.partial(scale_kernel, len(helds), first), out_sh...  2.8 us
  transfers between devices with their start and end apart: 17, of which 3 were waited for; matrix products, arithmetic and copies ran while one was open for 0% of the time, Pallas kernels for 34%

profile of v2, /device:TPU:0, one launch (start us, length us, event | category | flops | bytes accessed | tf_op | source)
XLA Modules:
  0.0 73.5 jit_solution(1453579391681998151)
XLA Ops:
  1.3 0.6 copy-done.2
  1.9 6.2 %attention.1 = (bf16[16,4096]{1,0:T(8,128)(2,1)S(1)}, bf16[4,4096]{1,0:T(4,128)(2,1)}, f32[4096,512]{1,0:T(8,128)S(1)}) custom-call(s32[16]{0:T(128)S(1)} %bitcast.9, s32[1]{0:T(128)S(6)} %copy.38.length_ref, bf16[4,16384]{1,0:T(4,128)(2,1)} %bitcast.12, bf16[16,64,256]{2,1,0:T(8,128)(2,1)} %bitcast.10, bf16[16,64,256]{2,1,0:T(8,128)(2,1)} %bitcast.11, ...), custom_call_target="tpu_custom_call" | custom-call | flops 67108864 | bytes 12582912 | tf_op jit(solution)/shard_map/attention/pallas_call | solution.py:249
  8.1 0.0 copy-start
  8.1 4.0 %collective-permute-start.2 = (bf16[16,4096]{1,0:T(8,128)(2,1)S(1)}, bf16[16,4096]{1,0:T(8,128)(2,1)S(1)}, u32[]{:S(2)}, u32[]{:S(2)}) collective-permute-start(bf16[16,4096]{1,0:T(8,128)(2,1)S(1)} %get-tuple-element.35.token_ref.refs_0_), channel_id=1, source_target_pairs={{0,24},{4,28},{8,16},{12,20},{16,8},{20,12},{24,0},{28,4},{1,25},{... | collective-permute-start | bytes 393224 | tf_op jit(solution)/shard_map/ppermute | solution.py:142
  12.1 0.5 collective-permute-start.1
  12.6 0.1 collective-permute-start
  12.7 5.9 %load_weight.2 = (f32[4096,1024]{1,0:T(8,128)S(1)}, f32[8,128]{1,0:T(8,128)S(1)}) custom-call(f32[4096,2048]{1,0:T(8,128)} %weight_ref.7, bf16[16,4096]{1,0:T(8,128)(2,1)S(1)} %get-tuple-element.35.token_ref.refs_0_), custom_call_target="tpu_custom_call" | custom-call | bytes 16777216 | tf_op jit(solution)/shard_map/load_weight/pallas_call | solution.py:313
  18.7 0.0 collective-permute-done.2.refs_3_
  18.8 0.1 collective-permute-start.3
  18.8 1.9 %collective-permute-done.3.refs_1_ = bf16[64,4096]{1,0:T(8,128)(2,1)S(1)} collective-permute-done((bf16[64,4096]{1,0:T(8,128)(2,1)S(1)}, bf16[64,4096]{1,0:T(8,128)(2,1)S(1)}, u32[]{:S(2)}, u32[]{:S(2)}) %collective-permute-start.3) | collective-permute-done | bytes 524320 | tf_op jit(solution)/shard_map/ppermute | solution.py:142
  20.7 4.8 %partial_logits.1 = (bf16[128,4096]{1,0:T(8,128)(2,1)S(1)}, f32[32,2048]{1,0:T(8,128)S(1)}, f32[128,128]{1,0:T(8,128)S(1)}, s16[32,2176]{1,0:T(8,128)(2,1)S(1)},...) custom-call(bf16[64,4096]{1,0:T(8,128)(2,1)S(1)} %stacked_rows.1.refs_0_, ...), custom_call_target="tpu_custom_call" | custom-call | flops 6442450944 | bytes 33554432 | tf_op jit(solution)/shard_map/partial_logits/pallas_call | solution.py:443
  25.5 3.1 %collective-permute-start.4 = (s16[32,2176]{1,0:T(8,128)(2,1)S(1)}, s16[32,2176]{1,0:T(8,128)(2,1)S(1)}, u32[]{:S(2)}, u32[]{:S(2)}) collective-permute-start(s16[32,2176]{1,0:T(8,128)(2,1)S(1)} %get-tuple-element.42), channel_id=1, source_target_pairs={{0,2},{1,3},{2,0},{3,1},{4,6},{5,7},{6,4},{7,5},{8,10},{9,11},{10,... | collective-permute-start | bytes 417800 | tf_op jit(solution)/shard_map/ppermute | solution.py:142
  28.6 1.6 %collective-permute-start.5 = (s16[32,2176]{1,0:T(8,128)(2,1)S(1)}, s16[32,2176]{1,0:T(8,128)(2,1)S(1)}, u32[]{:S(2)}, u32[]{:S(2)}) collective-permute-start(s16[32,2176]{1,0:T(8,128)(2,1)S(1)} %get-tuple-element.43), channel_id=1, source_target_pairs={{0,1},{1,0},{2,3},{3,2},{4,5},{5,4},{6,7},{7,6},{8,9},{9,8},{10,11... | collective-permute-start | bytes 417800 | tf_op jit(solution)/shard_map/ppermute | solution.py:142
  30.1 0.9 %turned_rows.1.refs_4_.turned_ref = f32[4096,128]{1,0:T(8,128)S(1)} custom-call(bf16[128,4096]{1,0:T(8,128)(2,1)S(1)} %get-tuple-element.39.x_ref, f32[1,4096]{1,0:T(1,128)S(1)} %bitcast.8), custom_call_target="tpu_custom_call" | custom-call | flops 4096 | bytes 4096 | tf_op jit(solution)/shard_map/turned_rows/pallas_call | solution.py:604
  31.1 9.6 %load_weight.3 = (f32[4096,768]{1,0:T(8,128)S(1)}, f32[4096,1024]{1,0:T(8,128)S(1)}, f32[8,128]{1,0:T(8,128)S(1)}) custom-call(f32[4096,2048]{1,0:T(8,128)} %weight_ref.7, f32[32,2048]{1,0:T(8,128)S(1)} %get-tuple-element.40.token_ref.own_ref), custom_call_target="tpu_custom_call" | custom-call | bytes 29360128 | tf_op jit(solution)/shard_map/load_weight/pallas_call | solution.py:313
  40.7 0.0 copy-start.1
  40.7 0.0 copy-start.3
  40.7 0.4 local_softmax.1
  41.1 3.9 %collective-permute-start.12 = (bf16[32,896]{1,0:T(8,128)(2,1)S(1)}, bf16[32,896]{1,0:T(8,128)(2,1)S(1)}, u32[]{:S(2)}, u32[]{:S(2)}) collective-permute-start(bf16[32,896]{1,0:T(8,128)(2,1)S(1)} %get-tuple-element.54.refs_0_.refs_2_), channel_id=1, source_target_pairs={{0,3},{1,2},{2,1},{3,0},{4,7},{5,6},{6,5},{7,4},{8,11},{9,10},{10,... | collective-permute-start | bytes 172040 | tf_op jit(solution)/shard_map/ppermute | solution.py:142
  45.0 0.6 collective-permute-start.10
  45.7 2.8 %scaled_rows.1 = (bf16[4096,256]{1,0:T(8,128)(2,1)S(1)}, s32[128,128]{1,0:T(8,128)S(1)}, f32[4096,768]{1,0:T(8,128)S(1)}, f32[4096,1024]{1,0:T(8,128)S(1)}, f32[4096,256]{1,0:T(8,128)S(1)}) custom-call(f32[4096,128]{1,0:T(8,128)S(1)} %turned_rows.1.refs_4_.turned_ref, ...), custom_call_target="tpu_custom_call", output_to_operand_aliasing={{2}: (5, {}), {3}: (6, {})} | custom-call | flops 65536 | bytes 65536 | tf_op jit(solution)/shard_map/scaled_rows/pallas_call | solution.py:648
  48.5 2.0 %collective-permute-done.11.refs_2_.refs_4_ = bf16[32,896]{1,0:T(8,128)(2,1)S(1)} collective-permute-done((bf16[32,896]{1,0:T(8,128)(2,1)S(1)}, bf16[32,896]{1,0:T(8,128)(2,1)S(1)}, u32[]{:S(2)}, u32[]{:S(2)}) %collective-permute-start.11) | collective-permute-done | bytes 57376 | tf_op jit(solution)/shard_map/ppermute | solution.py:142
  50.5 0.2 row_stats.1
  50.7 0.0 collective-permute-start.13
  50.8 1.2 %collective-permute-done.13.second_ref = f32[8,128]{1,0:T(8,128)S(1)} collective-permute-done((f32[8,128]{1,0:T(8,128)S(1)}, f32[8,128]{1,0:T(8,128)S(1)}, u32[]{:S(2)}, u32[]{:S(2)}) %collective-permute-start.13) | collective-permute-done | bytes 4128 | tf_op jit(solution)/shard_map/ppermute | solution.py:142
  51.9 2.5 %collective-permute-start.16 = (f32[8,128]{1,0:T(8,128)S(1)}, f32[8,128]{1,0:T(8,128)S(1)}, u32[]{:S(2)}, u32[]{:S(2)}) collective-permute-start(f32[8,128]{1,0:T(8,128)S(1)} %pair_stats.1.refs_7_), channel_id=1, source_target_pairs={{0,24},{4,28},{8,16},{12,20},{16,8},{20,12},{24,0},{28,4},{1,25},{... | collective-permute-start | bytes 12296 | tf_op jit(solution)/shard_map/ppermute | solution.py:142
  54.4 0.6 collective-permute-start.15
  55.0 0.5 collective-permute-start.14
  55.5 2.5 %collective-permute-start.9 = (bf16[32,1280]{1,0:T(8,128)(2,1)S(1)}, bf16[32,1280]{1,0:T(8,128)(2,1)S(1)}, u32[]{:S(2)}, u32[]{:S(2)}) collective-permute-start(bf16[32,1280]{1,0:T(8,128)(2,1)S(1)} %get-tuple-element.53.refs_2_), channel_id=1, source_target_pairs={{0,3},{1,2},{2,1},{3,0},{4,7},{5,6},{6,5},{7,4},{8,11},{9,10},{10,... | collective-permute-start | bytes 245768 | tf_op jit(solution)/shard_map/ppermute | solution.py:142
  58.0 1.8 %collective-permute-start.7 = (bf16[32,1280]{1,0:T(8,128)(2,1)S(1)}, bf16[32,1280]{1,0:T(8,128)(2,1)S(1)}, u32[]{:S(2)}, u32[]{:S(2)}) collective-permute-start(bf16[32,1280]{1,0:T(8,128)(2,1)S(1)} %get-tuple-element.53.refs_2_), channel_id=1, source_target_pairs={{0,1},{1,0},{2,3},{3,2},{4,5},{5,4},{6,7},{7,6},{8,9},{9,8},{10,11... | collective-permute-start | bytes 245768 | tf_op jit(solution)/shard_map/ppermute | solution.py:142
  59.9 5.6 %weight_update.2 = (f32[4096,2048]{1,0:T(8,128)}, f32[4096,768]{1,0:T(8,128)S(1)}, f32[4096,1024]{1,0:T(8,128)S(1)}, f32[4096,256]{1,0:T(8,128)S(1)}) custom-call(bf16[4096,256]{1,0:T(8,128)(2,1)S(1)} %get-tuple-element.51.refs_0_, s32[128,128]{1,0:T(8,128)S(1)} %get-tuple-element.52.refs_1_, ...), custom_call_target="tpu_custom_call", output_to_operand_aliasing={{1}: (11, {}), {2}: (12, {}), {3}: (13, {})} | custom-call | flops 1610612736 | bytes 12582912 | tf_op jit(solution)/shard_map/weight_update/pallas_call | solution.py:740
  65.6 8.0 %weight_update.3 = (f32[4096,2048]{1,0:T(8,128)}, f32[4096,1024]{1,0:T(8,128)S(1)}, f32[4096,256]{1,0:T(8,128)S(1)}) custom-call(bf16[4096,256]{1,0:T(8,128)(2,1)S(1)} %get-tuple-element.51.refs_0_, s32[128,128]{1,0:T(8,128)S(1)} %get-tuple-element.52.refs_1_, ...), custom_call_target="tpu_custom_call", output_to_operand_aliasing={{1}: (12, {}), {2}: (13, {}), {0}: (11, {})} | custom-call | flops 2684354560 | bytes 20971520 | tf_op jit(solution)/shard_map/weight_update/pallas_call | solution.py:740
  (22 shorter events, 0.1 us)
Async XLA Ops:
  1.3 0.7 copy-start.2
  8.1 12.6 %copy-start = (f32[4096]{0:T(1024)S(1)}, f32[4096]{0:T(1024)}, u32[]{:S(2)}) copy-start(f32[4096]{0:T(1024)} %param.16) | copy-start | bytes 49156
  8.1 10.5 %collective-permute-start.2 = (bf16[16,4096]{1,0:T(8,128)(2,1)S(1)}, bf16[16,4096]{1,0:T(8,128)(2,1)S(1)}, u32[]{:S(2)}, u32[]{:S(2)}) collective-permute-start(bf16[16,4096]{1,0:T(8,128)(2,1)S(1)} %get-tuple-element.35.token_ref.refs_0_), channel_id=1, source_target_pairs={{0,24},{4,28},{8,16},{12,20},{16,8},{20,12},{24,0},{28,4},{1,25},{... | collective-permute-start | bytes 393224 | tf_op jit(solution)/shard_map/ppermute | solution.py:142
  12.1 6.6 %collective-permute-start.1 = (bf16[16,4096]{1,0:T(8,128)(2,1)S(1)}, bf16[16,4096]{1,0:T(8,128)(2,1)S(1)}, u32[]{:S(2)}, u32[]{:S(2)}) collective-permute-start(bf16[16,4096]{1,0:T(8,128)(2,1)S(1)} %get-tuple-element.35.token_ref.refs_0_), channel_id=1, source_target_pairs={{0,16},{4,20},{8,24},{12,28},{16,0},{20,4},{24,8},{28,12},{1,17},{... | collective-permute-start | bytes 393224 | tf_op jit(solution)/shard_map/ppermute | solution.py:142
  12.6 6.1 %collective-permute-start = (bf16[16,4096]{1,0:T(8,128)(2,1)S(1)}, bf16[16,4096]{1,0:T(8,128)(2,1)S(1)}, u32[]{:S(2)}, u32[]{:S(2)}) collective-permute-start(bf16[16,4096]{1,0:T(8,128)(2,1)S(1)} %get-tuple-element.35.token_ref.refs_0_), channel_id=1, source_target_pairs={{0,8},{4,12},{8,0},{12,4},{16,24},{20,28},{24,16},{28,20},{1,9},{5... | collective-permute-start | bytes 393224 | tf_op jit(solution)/shard_map/ppermute | solution.py:142
  18.8 2.0 %collective-permute-start.3 = (bf16[64,4096]{1,0:T(8,128)(2,1)S(1)}, bf16[64,4096]{1,0:T(8,128)(2,1)S(1)}, u32[]{:S(2)}, u32[]{:S(2)}) collective-permute-start(bf16[64,4096]{1,0:T(8,128)(2,1)S(1)} %stacked_rows.1.refs_0_), channel_id=1, source_target_pairs={{0,4},{4,0},{8,12},{12,8},{16,20},{20,16},{24,28},{28,24},{1,5},{5... | collective-permute-start | bytes 1572872 | tf_op jit(solution)/shard_map/ppermute | solution.py:142
  25.5 15.2 %collective-permute-start.4 = (s16[32,2176]{1,0:T(8,128)(2,1)S(1)}, s16[32,2176]{1,0:T(8,128)(2,1)S(1)}, u32[]{:S(2)}, u32[]{:S(2)}) collective-permute-start(s16[32,2176]{1,0:T(8,128)(2,1)S(1)} %get-tuple-element.42), channel_id=1, source_target_pairs={{0,2},{1,3},{2,0},{3,1},{4,6},{5,7},{6,4},{7,5},{8,10},{9,11},{10,... | collective-permute-start | bytes 417800 | tf_op jit(solution)/shard_map/ppermute | solution.py:142
  28.6 12.1 %collective-permute-start.5 = (s16[32,2176]{1,0:T(8,128)(2,1)S(1)}, s16[32,2176]{1,0:T(8,128)(2,1)S(1)}, u32[]{:S(2)}, u32[]{:S(2)}) collective-permute-start(s16[32,2176]{1,0:T(8,128)(2,1)S(1)} %get-tuple-element.43), channel_id=1, source_target_pairs={{0,1},{1,0},{2,3},{3,2},{4,5},{5,4},{6,7},{7,6},{8,9},{9,8},{10,11... | collective-permute-start | bytes 417800 | tf_op jit(solution)/shard_map/ppermute | solution.py:142
  30.1 10.6 %collective-permute-start.6 = (s16[32,2176]{1,0:T(8,128)(2,1)S(1)}, s16[32,2176]{1,0:T(8,128)(2,1)S(1)}, u32[]{:S(2)}, u32[]{:S(2)}) collective-permute-start(s16[32,2176]{1,0:T(8,128)(2,1)S(1)} %get-tuple-element.44), channel_id=1, source_target_pairs={{0,3},{1,2},{2,1},{3,0},{4,7},{5,6},{6,5},{7,4},{8,11},{9,10},{10,... | collective-permute-start | bytes 417800 | tf_op jit(solution)/shard_map/ppermute | solution.py:142
  40.7 5.0 %copy-start.1 = (s32[8,16]{1,0:T(8,128)S(1)}, s32[8,16]{1,0:T(8,128)}, u32[]{:S(2)}) copy-start(s32[8,16]{1,0:T(8,128)} %targets_ref.1) | copy-start | bytes 1540
  40.7 4.9 %copy-start.3 = (s32[8]{0:T(128)S(1)}, s32[8]{0:T(128)}, u32[]{:S(2)}) copy-start(s32[8]{0:T(128)} %accepted_ref.1) | copy-start | bytes 100
  41.1 7.3 %collective-permute-start.12 = (bf16[32,896]{1,0:T(8,128)(2,1)S(1)}, bf16[32,896]{1,0:T(8,128)(2,1)S(1)}, u32[]{:S(2)}, u32[]{:S(2)}) collective-permute-start(bf16[32,896]{1,0:T(8,128)(2,1)S(1)} %get-tuple-element.54.refs_0_.refs_2_), channel_id=1, source_target_pairs={{0,3},{1,2},{2,1},{3,0},{4,7},{5,6},{6,5},{7,4},{8,11},{9,10},{10,... | collective-permute-start | bytes 172040 | tf_op jit(solution)/shard_map/ppermute | solution.py:142
  45.0 5.5 %collective-permute-start.11 = (bf16[32,896]{1,0:T(8,128)(2,1)S(1)}, bf16[32,896]{1,0:T(8,128)(2,1)S(1)}, u32[]{:S(2)}, u32[]{:S(2)}) collective-permute-start(bf16[32,896]{1,0:T(8,128)(2,1)S(1)} %get-tuple-element.54.refs_0_.refs_2_), channel_id=1, source_target_pairs={{0,2},{1,3},{2,0},{3,1},{4,6},{5,7},{6,4},{7,5},{8,10},{9,11},{10,... | collective-permute-start | bytes 172040 | tf_op jit(solution)/shard_map/ppermute | solution.py:142
  45.0 5.5 %collective-permute-start.10 = (bf16[32,896]{1,0:T(8,128)(2,1)S(1)}, bf16[32,896]{1,0:T(8,128)(2,1)S(1)}, u32[]{:S(2)}, u32[]{:S(2)}) collective-permute-start(bf16[32,896]{1,0:T(8,128)(2,1)S(1)} %get-tuple-element.54.refs_0_.refs_2_), channel_id=1, source_target_pairs={{0,1},{1,0},{2,3},{3,2},{4,5},{5,4},{6,7},{7,6},{8,9},{9,8},{10,11... | collective-permute-start | bytes 172040 | tf_op jit(solution)/shard_map/ppermute | solution.py:142
  50.7 1.2 %collective-permute-start.13 = (f32[8,128]{1,0:T(8,128)S(1)}, f32[8,128]{1,0:T(8,128)S(1)}, u32[]{:S(2)}, u32[]{:S(2)}) collective-permute-start(f32[8,128]{1,0:T(8,128)S(1)} %get-tuple-element.58.first_ref.refs_6_), channel_id=1, source_target_pairs={{0,4},{4,0},{8,12},{12,8},{16,20},{20,16},{24,28},{28,24},{1,5},{5... | collective-permute-start | bytes 12296 | tf_op jit(solution)/shard_map/ppermute | solution.py:142
  51.9 6.1 %collective-permute-start.16 = (f32[8,128]{1,0:T(8,128)S(1)}, f32[8,128]{1,0:T(8,128)S(1)}, u32[]{:S(2)}, u32[]{:S(2)}) collective-permute-start(f32[8,128]{1,0:T(8,128)S(1)} %pair_stats.1.refs_7_), channel_id=1, source_target_pairs={{0,24},{4,28},{8,16},{12,20},{16,8},{20,12},{24,0},{28,4},{1,25},{... | collective-permute-start | bytes 12296 | tf_op jit(solution)/shard_map/ppermute | solution.py:142
  54.4 5.5 %collective-permute-start.15 = (f32[8,128]{1,0:T(8,128)S(1)}, f32[8,128]{1,0:T(8,128)S(1)}, u32[]{:S(2)}, u32[]{:S(2)}) collective-permute-start(f32[8,128]{1,0:T(8,128)S(1)} %pair_stats.1.refs_7_), channel_id=1, source_target_pairs={{0,16},{4,20},{8,24},{12,28},{16,0},{20,4},{24,8},{28,12},{1,17},{... | collective-permute-start | bytes 12296 | tf_op jit(solution)/shard_map/ppermute | solution.py:142
  55.0 4.9 %collective-permute-start.14 = (f32[8,128]{1,0:T(8,128)S(1)}, f32[8,128]{1,0:T(8,128)S(1)}, u32[]{:S(2)}, u32[]{:S(2)}) collective-permute-start(f32[8,128]{1,0:T(8,128)S(1)} %pair_stats.1.refs_7_), channel_id=1, source_target_pairs={{0,8},{4,12},{8,0},{12,4},{16,24},{20,28},{24,16},{28,20},{1,9},{5... | collective-permute-start | bytes 12296 | tf_op jit(solution)/shard_map/ppermute | solution.py:142
  55.5 10.0 %collective-permute-start.9 = (bf16[32,1280]{1,0:T(8,128)(2,1)S(1)}, bf16[32,1280]{1,0:T(8,128)(2,1)S(1)}, u32[]{:S(2)}, u32[]{:S(2)}) collective-permute-start(bf16[32,1280]{1,0:T(8,128)(2,1)S(1)} %get-tuple-element.53.refs_2_), channel_id=1, source_target_pairs={{0,3},{1,2},{2,1},{3,0},{4,7},{5,6},{6,5},{7,4},{8,11},{9,10},{10,... | collective-permute-start | bytes 245768 | tf_op jit(solution)/shard_map/ppermute | solution.py:142
  58.0 7.5 %collective-permute-start.8 = (bf16[32,1280]{1,0:T(8,128)(2,1)S(1)}, bf16[32,1280]{1,0:T(8,128)(2,1)S(1)}, u32[]{:S(2)}, u32[]{:S(2)}) collective-permute-start(bf16[32,1280]{1,0:T(8,128)(2,1)S(1)} %get-tuple-element.53.refs_2_), channel_id=1, source_target_pairs={{0,2},{1,3},{2,0},{3,1},{4,6},{5,7},{6,4},{7,5},{8,10},{9,11},{10,... | collective-permute-start | bytes 245768 | tf_op jit(solution)/shard_map/ppermute | solution.py:142
  58.0 7.5 %collective-permute-start.7 = (bf16[32,1280]{1,0:T(8,128)(2,1)S(1)}, bf16[32,1280]{1,0:T(8,128)(2,1)S(1)}, u32[]{:S(2)}, u32[]{:S(2)}) collective-permute-start(bf16[32,1280]{1,0:T(8,128)(2,1)S(1)} %get-tuple-element.53.refs_2_), channel_id=1, source_target_pairs={{0,1},{1,0},{2,3},{3,2},{4,5},{5,4},{6,7},{7,6},{8,9},{9,8},{10,11... | collective-permute-start | bytes 245768 | tf_op jit(solution)/shard_map/ppermute | solution.py:142

commit v3 on v2

--- a/solution.py
+++ b/solution.py
@@ -18,7 +18,7 @@
 TILE = 512
 SUM_ORDER = (2, 1, 3)
 BACK_ORDER = (1, 2, 3)
-HEIGHT = 256
+HEIGHT = 512
 HELD = (512, 1024)
 AGAIN = (768, 1024)
 bf16 = jnp.bfloat16
@@ -177,6 +177,9 @@
     group = HQ // KVH
     span = query_buf.shape[1]
     start = pl.multiple_of(lax.axis_index("tp") * span, span)
+    weight_copies = column_copies(weight_ref, held_ref, weight_sem, 0)
+    for copy in weight_copies:
+        copy.start()
     query_copy = pltpu.make_async_copy(queries_ref.at[:, pl.ds(start, span)], query_buf, query_sem)
     query_copy.start()
     key_copies, value_copies = [], []
@@ -200,11 +203,8 @@
             queries[:, (head * group + g) * HD : (head * group + g + 1) * HD] for g in range(group)
         ]
         stacked.append(jnp.concatenate(parts, axis=0).astype(bf16))
-    for copy in key_copies + value_copies:
+    for copy in key_copies:
         copy.wait()
-    weight_copies = column_copies(weight_ref, held_ref, weight_sem, 0)
-    for copy in weight_copies:
-        copy.start()
     shape = (group * steps, pages * slots)
     step = lax.broadcasted_iota(jnp.int32, shape, 0) % steps
     position = lax.broadcasted_iota(jnp.int32, shape, 1)
@@ -221,6 +221,8 @@
         expo = jnp.where(valid, jnp.exp(scores - top), 0.0)
         totals.append(jnp.sum(expo, axis=-1, keepdims=True))
         expos.append(jnp.concatenate(split2(expo), axis=0))
+    for copy in value_copies:
+        copy.wait()
     history_copy.wait()
     for head in range(kv_local):
         both = jnp.dot(
@@ -279,7 +281,7 @@
             flops=4 * 64 * 1024 * 256, bytes_accessed=12 * MIB, transcendentals=131072
         ),
         name="attention",
-    )(table, length, *(in_hbm(part) for part in (queries, keys, values, history, weight)))
+    )(in_hbm(table), length, *(in_hbm(part) for part in (queries, keys, values, history, weight)))
 
 
 def column_copies(source, target, sems, first, width=256):

time: 73.8 us -> 72.8 us (0.986)
  no operation moved by 1% of the time
where the time goes in v3:
time: 72.8 us; the launch traced here: 72.6 us
  Pallas kernels  44.2 us (61%)
  starting transfers between devices  21.8 us (30%)
  waiting for transfers between devices  5.1 us (7%)
  between operations  1.47 us (2%)
    ppermute x17, starting transfers between devices, exchange(): return lax.ppermute(value, axis, pairs)  21.8 us
    pallas_call x2, Pallas kernels, run_load(): pl.pallas_call(functools.partial(load_kernel, first, len(widths)), out_sh...  15.5 us
    pallas_call x2, Pallas kernels, run_update(): pl.pallas_call(functools.partial(update_kernel, n_tp, n_held, len(kept),...  13.3 us
    pallas_call x1, Pallas kernels, run_attention(): pl.pallas_call(functools.partial(attention_kernel, kv_local), out_shape=(...  6.18 us
    ppermute x17, waiting for transfers between devices, exchange(): return lax.ppermute(value, axis, pairs)  5.1 us
    pallas_call x1, Pallas kernels, run_logits(): pl.pallas_call(functools.partial(logits_kernel, n_rep, n_tp), grid=(tiles...  4.77 us
    pallas_call x1, Pallas kernels, run_scale(): pl.pallas_call(functools.partial(scale_kernel, len(helds), first), out_sh...  2.8 us
  transfers between devices with their start and end apart: 17, of which 3 were waited for; matrix products, arithmetic and copies ran while one was open for 0% of the time, Pallas kernels for 34%

profile of v3, /device:TPU:0, one launch (start us, length us, event | category | flops | bytes accessed | tf_op | source)
XLA Modules:
  0.0 72.6 jit_solution(5665905560285861771)
XLA Ops:
  1.3 6.2 %attention.1 = (bf16[16,4096]{1,0:T(8,128)(2,1)S(1)}, bf16[4,4096]{1,0:T(4,128)(2,1)}, f32[4096,512]{1,0:T(8,128)S(1)}) custom-call(s32[16]{0:T(128)} %bitcast.13, s32[1]{0:T(128)S(6)} %copy.38.length_ref, bf16[4,16384]{1,0:T(4,128)(2,1)} %bitcast.11, bf16[16,64,256]{2,1,0:T(8,128)(2,1)} %bitcast.9, bf16[16,64,256]{2,1,0:T(8,128)(2,1)} %bitcast.10, ...), custom_call_target="tpu_custom_call" | custom-call | flops 67108864 | bytes 12582912 | tf_op jit(solution)/shard_map/attention/pallas_call | solution.py:251
  7.5 0.0 copy-start
  7.5 4.0 %collective-permute-start.2 = (bf16[16,4096]{1,0:T(8,128)(2,1)S(1)}, bf16[16,4096]{1,0:T(8,128)(2,1)S(1)}, u32[]{:S(2)}, u32[]{:S(2)}) collective-permute-start(bf16[16,4096]{1,0:T(8,128)(2,1)S(1)} %get-tuple-element.35.token_ref.refs_0_), channel_id=1, source_target_pairs={{0,24},{4,28},{8,16},{12,20},{16,8},{20,12},{24,0},{28,4},{1,25},{... | collective-permute-start | bytes 393224 | tf_op jit(solution)/shard_map/ppermute | solution.py:142
  11.4 0.5 collective-permute-start.1
  11.9 0.1 collective-permute-start
  12.1 5.9 %load_weight.2 = (f32[4096,1024]{1,0:T(8,128)S(1)}, f32[8,128]{1,0:T(8,128)S(1)}) custom-call(f32[4096,2048]{1,0:T(8,128)} %weight_ref.7, bf16[16,4096]{1,0:T(8,128)(2,1)S(1)} %get-tuple-element.35.token_ref.refs_0_), custom_call_target="tpu_custom_call" | custom-call | bytes 16777216 | tf_op jit(solution)/shard_map/load_weight/pallas_call | solution.py:315
  18.0 0.0 collective-permute-done.1.refs_2_
  18.0 0.0 collective-permute-done.refs_1_
  18.1 0.1 collective-permute-start.3
  18.2 1.9 %collective-permute-done.3.refs_1_ = bf16[64,4096]{1,0:T(8,128)(2,1)S(1)} collective-permute-done((bf16[64,4096]{1,0:T(8,128)(2,1)S(1)}, bf16[64,4096]{1,0:T(8,128)(2,1)S(1)}, u32[]{:S(2)}, u32[]{:S(2)}) %collective-permute-start.3) | collective-permute-done | bytes 524320 | tf_op jit(solution)/shard_map/ppermute | solution.py:142
  20.1 4.8 %partial_logits.1 = (bf16[128,4096]{1,0:T(8,128)(2,1)S(1)}, f32[32,2048]{1,0:T(8,128)S(1)}, f32[128,128]{1,0:T(8,128)S(1)}, s16[32,2176]{1,0:T(8,128)(2,1)S(1)},...) custom-call(bf16[64,4096]{1,0:T(8,128)(2,1)S(1)} %stacked_rows.1.refs_0_, ...), custom_call_target="tpu_custom_call" | custom-call | flops 6442450944 | bytes 33554432 | tf_op jit(solution)/shard_map/partial_logits/pallas_call | solution.py:445
  24.8 3.1 %collective-permute-start.4 = (s16[32,2176]{1,0:T(8,128)(2,1)S(1)}, s16[32,2176]{1,0:T(8,128)(2,1)S(1)}, u32[]{:S(2)}, u32[]{:S(2)}) collective-permute-start(s16[32,2176]{1,0:T(8,128)(2,1)S(1)} %get-tuple-element.42), channel_id=1, source_target_pairs={{0,2},{1,3},{2,0},{3,1},{4,6},{5,7},{6,4},{7,5},{8,10},{9,11},{10,... | collective-permute-start | bytes 417800 | tf_op jit(solution)/shard_map/ppermute | solution.py:142
  27.9 1.6 %collective-permute-start.5 = (s16[32,2176]{1,0:T(8,128)(2,1)S(1)}, s16[32,2176]{1,0:T(8,128)(2,1)S(1)}, u32[]{:S(2)}, u32[]{:S(2)}) collective-permute-start(s16[32,2176]{1,0:T(8,128)(2,1)S(1)} %get-tuple-element.43), channel_id=1, source_target_pairs={{0,1},{1,0},{2,3},{3,2},{4,5},{5,4},{6,7},{7,6},{8,9},{9,8},{10,11... | collective-permute-start | bytes 417800 | tf_op jit(solution)/shard_map/ppermute | solution.py:142
  29.5 0.9 %turned_rows.1.refs_4_.turned_ref = f32[4096,128]{1,0:T(8,128)S(1)} custom-call(bf16[128,4096]{1,0:T(8,128)(2,1)S(1)} %get-tuple-element.39.x_ref, f32[1,4096]{1,0:T(1,128)S(1)} %bitcast.8), custom_call_target="tpu_custom_call" | custom-call | flops 4096 | bytes 4096 | tf_op jit(solution)/shard_map/turned_rows/pallas_call | solution.py:606
  30.4 9.6 %load_weight.3 = (f32[4096,768]{1,0:T(8,128)S(1)}, f32[4096,1024]{1,0:T(8,128)S(1)}, f32[8,128]{1,0:T(8,128)S(1)}) custom-call(f32[4096,2048]{1,0:T(8,128)} %weight_ref.7, f32[32,2048]{1,0:T(8,128)S(1)} %get-tuple-element.40.token_ref.own_ref), custom_call_target="tpu_custom_call" | custom-call | bytes 29360128 | tf_op jit(solution)/shard_map/load_weight/pallas_call | solution.py:315
  40.1 0.0 copy-start.1
  40.1 0.0 copy-start.2
  40.1 0.4 local_softmax.1
  40.5 3.9 %collective-permute-start.12 = (bf16[32,896]{1,0:T(8,128)(2,1)S(1)}, bf16[32,896]{1,0:T(8,128)(2,1)S(1)}, u32[]{:S(2)}, u32[]{:S(2)}) collective-permute-start(bf16[32,896]{1,0:T(8,128)(2,1)S(1)} %get-tuple-element.54.refs_0_.refs_2_), channel_id=1, source_target_pairs={{0,3},{1,2},{2,1},{3,0},{4,7},{5,6},{6,5},{7,4},{8,11},{9,10},{10,... | collective-permute-start | bytes 172040 | tf_op jit(solution)/shard_map/ppermute | solution.py:142
  44.4 0.6 collective-permute-start.10
  45.0 2.8 %scaled_rows.1 = (bf16[4096,256]{1,0:T(8,128)(2,1)S(1)}, s32[128,128]{1,0:T(8,128)S(1)}, f32[4096,768]{1,0:T(8,128)S(1)}, f32[4096,1024]{1,0:T(8,128)S(1)}, f32[4096,256]{1,0:T(8,128)S(1)}) custom-call(f32[4096,128]{1,0:T(8,128)S(1)} %turned_rows.1.refs_4_.turned_ref, ...), custom_call_target="tpu_custom_call", output_to_operand_aliasing={{2}: (5, {}), {3}: (6, {})} | custom-call | flops 65536 | bytes 65536 | tf_op jit(solution)/shard_map/scaled_rows/pallas_call | solution.py:650
  47.8 2.0 %collective-permute-done.11.refs_2_.refs_4_ = bf16[32,896]{1,0:T(8,128)(2,1)S(1)} collective-permute-done((bf16[32,896]{1,0:T(8,128)(2,1)S(1)}, bf16[32,896]{1,0:T(8,128)(2,1)S(1)}, u32[]{:S(2)}, u32[]{:S(2)}) %collective-permute-start.11) | collective-permute-done | bytes 57376 | tf_op jit(solution)/shard_map/ppermute | solution.py:142
  49.8 0.2 row_stats.1
  50.1 0.0 collective-permute-start.13
  50.1 1.2 %collective-permute-done.13.second_ref = f32[8,128]{1,0:T(8,128)S(1)} collective-permute-done((f32[8,128]{1,0:T(8,128)S(1)}, f32[8,128]{1,0:T(8,128)S(1)}, u32[]{:S(2)}, u32[]{:S(2)}) %collective-permute-start.13) | collective-permute-done | bytes 4128 | tf_op jit(solution)/shard_map/ppermute | solution.py:142
  51.3 2.5 %collective-permute-start.16 = (f32[8,128]{1,0:T(8,128)S(1)}, f32[8,128]{1,0:T(8,128)S(1)}, u32[]{:S(2)}, u32[]{:S(2)}) collective-permute-start(f32[8,128]{1,0:T(8,128)S(1)} %pair_stats.1.refs_7_), channel_id=1, source_target_pairs={{0,24},{4,28},{8,16},{12,20},{16,8},{20,12},{24,0},{28,4},{1,25},{... | collective-permute-start | bytes 12296 | tf_op jit(solution)/shard_map/ppermute | solution.py:142
  53.8 0.5 collective-permute-start.15
  54.3 0.5 collective-permute-start.14
  54.8 2.5 %collective-permute-start.9 = (bf16[32,1280]{1,0:T(8,128)(2,1)S(1)}, bf16[32,1280]{1,0:T(8,128)(2,1)S(1)}, u32[]{:S(2)}, u32[]{:S(2)}) collective-permute-start(bf16[32,1280]{1,0:T(8,128)(2,1)S(1)} %get-tuple-element.53.refs_2_), channel_id=1, source_target_pairs={{0,3},{1,2},{2,1},{3,0},{4,7},{5,6},{6,5},{7,4},{8,11},{9,10},{10,... | collective-permute-start | bytes 245768 | tf_op jit(solution)/shard_map/ppermute | solution.py:142
  57.4 1.8 %collective-permute-start.7 = (bf16[32,1280]{1,0:T(8,128)(2,1)S(1)}, bf16[32,1280]{1,0:T(8,128)(2,1)S(1)}, u32[]{:S(2)}, u32[]{:S(2)}) collective-permute-start(bf16[32,1280]{1,0:T(8,128)(2,1)S(1)} %get-tuple-element.53.refs_2_), channel_id=1, source_target_pairs={{0,1},{1,0},{2,3},{3,2},{4,5},{5,4},{6,7},{7,6},{8,9},{9,8},{10,11... | collective-permute-start | bytes 245768 | tf_op jit(solution)/shard_map/ppermute | solution.py:142
  59.2 5.3 %weight_update.2 = (f32[4096,2048]{1,0:T(8,128)}, f32[4096,768]{1,0:T(8,128)S(1)}, f32[4096,1024]{1,0:T(8,128)S(1)}, f32[4096,256]{1,0:T(8,128)S(1)}) custom-call(bf16[4096,256]{1,0:T(8,128)(2,1)S(1)} %get-tuple-element.51.refs_0_, s32[128,128]{1,0:T(8,128)S(1)} %get-tuple-element.52.refs_1_, ...), custom_call_target="tpu_custom_call", output_to_operand_aliasing={{1}: (11, {}), {2}: (12, {}), {3}: (13, {})} | custom-call | flops 1610612736 | bytes 12582912 | tf_op jit(solution)/shard_map/weight_update/pallas_call | solution.py:742
  64.6 8.0 %weight_update.3 = (f32[4096,2048]{1,0:T(8,128)}, f32[4096,1024]{1,0:T(8,128)S(1)}, f32[4096,256]{1,0:T(8,128)S(1)}) custom-call(bf16[4096,256]{1,0:T(8,128)(2,1)S(1)} %get-tuple-element.51.refs_0_, s32[128,128]{1,0:T(8,128)S(1)} %get-tuple-element.52.refs_1_, ...), custom_call_target="tpu_custom_call", output_to_operand_aliasing={{1}: (12, {}), {2}: (13, {}), {0}: (11, {})} | custom-call | flops 2684354560 | bytes 20971520 | tf_op jit(solution)/shard_map/weight_update/pallas_call | solution.py:742
  (20 shorter events, 0.1 us)
Async XLA Ops:
  7.5 12.6 %copy-start = (f32[4096]{0:T(1024)S(1)}, f32[4096]{0:T(1024)}, u32[]{:S(2)}) copy-start(f32[4096]{0:T(1024)} %param.16) | copy-start | bytes 49156
  7.5 10.5 %collective-permute-start.2 = (bf16[16,4096]{1,0:T(8,128)(2,1)S(1)}, bf16[16,4096]{1,0:T(8,128)(2,1)S(1)}, u32[]{:S(2)}, u32[]{:S(2)}) collective-permute-start(bf16[16,4096]{1,0:T(8,128)(2,1)S(1)} %get-tuple-element.35.token_ref.refs_0_), channel_id=1, source_target_pairs={{0,24},{4,28},{8,16},{12,20},{16,8},{20,12},{24,0},{28,4},{1,25},{... | collective-permute-start | bytes 393224 | tf_op jit(solution)/shard_map/ppermute | solution.py:142
  11.4 6.6 %collective-permute-start.1 = (bf16[16,4096]{1,0:T(8,128)(2,1)S(1)}, bf16[16,4096]{1,0:T(8,128)(2,1)S(1)}, u32[]{:S(2)}, u32[]{:S(2)}) collective-permute-start(bf16[16,4096]{1,0:T(8,128)(2,1)S(1)} %get-tuple-element.35.token_ref.refs_0_), channel_id=1, source_target_pairs={{0,16},{4,20},{8,24},{12,28},{16,0},{20,4},{24,8},{28,12},{1,17},{... | collective-permute-start | bytes 393224 | tf_op jit(solution)/shard_map/ppermute | solution.py:142
  11.9 6.1 %collective-permute-start = (bf16[16,4096]{1,0:T(8,128)(2,1)S(1)}, bf16[16,4096]{1,0:T(8,128)(2,1)S(1)}, u32[]{:S(2)}, u32[]{:S(2)}) collective-permute-start(bf16[16,4096]{1,0:T(8,128)(2,1)S(1)} %get-tuple-element.35.token_ref.refs_0_), channel_id=1, source_target_pairs={{0,8},{4,12},{8,0},{12,4},{16,24},{20,28},{24,16},{28,20},{1,9},{5... | collective-permute-start | bytes 393224 | tf_op jit(solution)/shard_map/ppermute | solution.py:142
  18.1 2.0 %collective-permute-start.3 = (bf16[64,4096]{1,0:T(8,128)(2,1)S(1)}, bf16[64,4096]{1,0:T(8,128)(2,1)S(1)}, u32[]{:S(2)}, u32[]{:S(2)}) collective-permute-start(bf16[64,4096]{1,0:T(8,128)(2,1)S(1)} %stacked_rows.1.refs_0_), channel_id=1, source_target_pairs={{0,4},{4,0},{8,12},{12,8},{16,20},{20,16},{24,28},{28,24},{1,5},{5... | collective-permute-start | bytes 1572872 | tf_op jit(solution)/shard_map/ppermute | solution.py:142
  24.8 15.2 %collective-permute-start.4 = (s16[32,2176]{1,0:T(8,128)(2,1)S(1)}, s16[32,2176]{1,0:T(8,128)(2,1)S(1)}, u32[]{:S(2)}, u32[]{:S(2)}) collective-permute-start(s16[32,2176]{1,0:T(8,128)(2,1)S(1)} %get-tuple-element.42), channel_id=1, source_target_pairs={{0,2},{1,3},{2,0},{3,1},{4,6},{5,7},{6,4},{7,5},{8,10},{9,11},{10,... | collective-permute-start | bytes 417800 | tf_op jit(solution)/shard_map/ppermute | solution.py:142
  27.9 12.1 %collective-permute-start.5 = (s16[32,2176]{1,0:T(8,128)(2,1)S(1)}, s16[32,2176]{1,0:T(8,128)(2,1)S(1)}, u32[]{:S(2)}, u32[]{:S(2)}) collective-permute-start(s16[32,2176]{1,0:T(8,128)(2,1)S(1)} %get-tuple-element.43), channel_id=1, source_target_pairs={{0,1},{1,0},{2,3},{3,2},{4,5},{5,4},{6,7},{7,6},{8,9},{9,8},{10,11... | collective-permute-start | bytes 417800 | tf_op jit(solution)/shard_map/ppermute | solution.py:142
  29.5 10.6 %collective-permute-start.6 = (s16[32,2176]{1,0:T(8,128)(2,1)S(1)}, s16[32,2176]{1,0:T(8,128)(2,1)S(1)}, u32[]{:S(2)}, u32[]{:S(2)}) collective-permute-start(s16[32,2176]{1,0:T(8,128)(2,1)S(1)} %get-tuple-element.44), channel_id=1, source_target_pairs={{0,3},{1,2},{2,1},{3,0},{4,7},{5,6},{6,5},{7,4},{8,11},{9,10},{10,... | collective-permute-start | bytes 417800 | tf_op jit(solution)/shard_map/ppermute | solution.py:142
  40.1 5.0 %copy-start.1 = (s32[8,16]{1,0:T(8,128)S(1)}, s32[8,16]{1,0:T(8,128)}, u32[]{:S(2)}) copy-start(s32[8,16]{1,0:T(8,128)} %targets_ref.1) | copy-start | bytes 1540
  40.1 4.9 %copy-start.2 = (s32[8]{0:T(128)S(1)}, s32[8]{0:T(128)}, u32[]{:S(2)}) copy-start(s32[8]{0:T(128)} %accepted_ref.1) | copy-start | bytes 100
  40.5 7.3 %collective-permute-start.12 = (bf16[32,896]{1,0:T(8,128)(2,1)S(1)}, bf16[32,896]{1,0:T(8,128)(2,1)S(1)}, u32[]{:S(2)}, u32[]{:S(2)}) collective-permute-start(bf16[32,896]{1,0:T(8,128)(2,1)S(1)} %get-tuple-element.54.refs_0_.refs_2_), channel_id=1, source_target_pairs={{0,3},{1,2},{2,1},{3,0},{4,7},{5,6},{6,5},{7,4},{8,11},{9,10},{10,... | collective-permute-start | bytes 172040 | tf_op jit(solution)/shard_map/ppermute | solution.py:142
  44.4 5.5 %collective-permute-start.11 = (bf16[32,896]{1,0:T(8,128)(2,1)S(1)}, bf16[32,896]{1,0:T(8,128)(2,1)S(1)}, u32[]{:S(2)}, u32[]{:S(2)}) collective-permute-start(bf16[32,896]{1,0:T(8,128)(2,1)S(1)} %get-tuple-element.54.refs_0_.refs_2_), channel_id=1, source_target_pairs={{0,2},{1,3},{2,0},{3,1},{4,6},{5,7},{6,4},{7,5},{8,10},{9,11},{10,... | collective-permute-start | bytes 172040 | tf_op jit(solution)/shard_map/ppermute | solution.py:142
  44.4 5.5 %collective-permute-start.10 = (bf16[32,896]{1,0:T(8,128)(2,1)S(1)}, bf16[32,896]{1,0:T(8,128)(2,1)S(1)}, u32[]{:S(2)}, u32[]{:S(2)}) collective-permute-start(bf16[32,896]{1,0:T(8,128)(2,1)S(1)} %get-tuple-element.54.refs_0_.refs_2_), channel_id=1, source_target_pairs={{0,1},{1,0},{2,3},{3,2},{4,5},{5,4},{6,7},{7,6},{8,9},{9,8},{10,11... | collective-permute-start | bytes 172040 | tf_op jit(solution)/shard_map/ppermute | solution.py:142
  50.1 1.2 %collective-permute-start.13 = (f32[8,128]{1,0:T(8,128)S(1)}, f32[8,128]{1,0:T(8,128)S(1)}, u32[]{:S(2)}, u32[]{:S(2)}) collective-permute-start(f32[8,128]{1,0:T(8,128)S(1)} %get-tuple-element.58.first_ref.refs_6_), channel_id=1, source_target_pairs={{0,4},{4,0},{8,12},{12,8},{16,20},{20,16},{24,28},{28,24},{1,5},{5... | collective-permute-start | bytes 12296 | tf_op jit(solution)/shard_map/ppermute | solution.py:142
  51.3 6.1 %collective-permute-start.16 = (f32[8,128]{1,0:T(8,128)S(1)}, f32[8,128]{1,0:T(8,128)S(1)}, u32[]{:S(2)}, u32[]{:S(2)}) collective-permute-start(f32[8,128]{1,0:T(8,128)S(1)} %pair_stats.1.refs_7_), channel_id=1, source_target_pairs={{0,24},{4,28},{8,16},{12,20},{16,8},{20,12},{24,0},{28,4},{1,25},{... | collective-permute-start | bytes 12296 | tf_op jit(solution)/shard_map/ppermute | solution.py:142
  53.8 5.4 %collective-permute-start.15 = (f32[8,128]{1,0:T(8,128)S(1)}, f32[8,128]{1,0:T(8,128)S(1)}, u32[]{:S(2)}, u32[]{:S(2)}) collective-permute-start(f32[8,128]{1,0:T(8,128)S(1)} %pair_stats.1.refs_7_), channel_id=1, source_target_pairs={{0,16},{4,20},{8,24},{12,28},{16,0},{20,4},{24,8},{28,12},{1,17},{... | collective-permute-start | bytes 12296 | tf_op jit(solution)/shard_map/ppermute | solution.py:142
  54.3 4.9 %collective-permute-start.14 = (f32[8,128]{1,0:T(8,128)S(1)}, f32[8,128]{1,0:T(8,128)S(1)}, u32[]{:S(2)}, u32[]{:S(2)}) collective-permute-start(f32[8,128]{1,0:T(8,128)S(1)} %pair_stats.1.refs_7_), channel_id=1, source_target_pairs={{0,8},{4,12},{8,0},{12,4},{16,24},{20,28},{24,16},{28,20},{1,9},{5... | collective-permute-start | bytes 12296 | tf_op jit(solution)/shard_map/ppermute | solution.py:142
  54.8 9.7 %collective-permute-start.9 = (bf16[32,1280]{1,0:T(8,128)(2,1)S(1)}, bf16[32,1280]{1,0:T(8,128)(2,1)S(1)}, u32[]{:S(2)}, u32[]{:S(2)}) collective-permute-start(bf16[32,1280]{1,0:T(8,128)(2,1)S(1)} %get-tuple-element.53.refs_2_), channel_id=1, source_target_pairs={{0,3},{1,2},{2,1},{3,0},{4,7},{5,6},{6,5},{7,4},{8,11},{9,10},{10,... | collective-permute-start | bytes 245768 | tf_op jit(solution)/shard_map/ppermute | solution.py:142
  57.4 7.2 %collective-permute-start.8 = (bf16[32,1280]{1,0:T(8,128)(2,1)S(1)}, bf16[32,1280]{1,0:T(8,128)(2,1)S(1)}, u32[]{:S(2)}, u32[]{:S(2)}) collective-permute-start(bf16[32,1280]{1,0:T(8,128)(2,1)S(1)} %get-tuple-element.53.refs_2_), channel_id=1, source_target_pairs={{0,2},{1,3},{2,0},{3,1},{4,6},{5,7},{6,4},{7,5},{8,10},{9,11},{10,... | collective-permute-start | bytes 245768 | tf_op jit(solution)/shard_map/ppermute | solution.py:142
  57.4 7.2 %collective-permute-start.7 = (bf16[32,1280]{1,0:T(8,128)(2,1)S(1)}, bf16[32,1280]{1,0:T(8,128)(2,1)S(1)}, u32[]{:S(2)}, u32[]{:S(2)}) collective-permute-start(bf16[32,1280]{1,0:T(8,128)(2,1)S(1)} %get-tuple-element.53.refs_2_), channel_id=1, source_target_pairs={{0,1},{1,0},{2,3},{3,2},{4,5},{5,4},{6,7},{7,6},{8,9},{9,8},{10,11... | collective-permute-start | bytes 245768 | tf_op jit(solution)/shard_map/ppermute | solution.py:142

commit v4 on v3

--- a/solution.py
+++ b/solution.py
@@ -798,7 +798,7 @@
     turned = run_turn(x, gain)
     received = [exchange(sends[k - 1], "tp", k) for k in SUM_ORDER]
     helds, loaded = run_load(draft_weight, own, 0, AGAIN)
-    left, right, scale, *helds = run_softmax(own, squares, received, (loaded, turned), helds)
+    left, right, scale, *helds = run_softmax(own, squares, received, (loaded,), helds)
     lefts = [left] + [exchange(left, "tp", k) for k in BACK_ORDER]
     scaled, target, *helds = run_scale(turned, scale, targets, accepted, draft_weight, helds)
     stat, *helds = run_stats(lefts, helds)

time: 72.8 us -> 71.9 us (0.988)
  waiting for transfers between devices: 5.1 us -> 3.78 us
    ppermute x17, waiting for transfers between devices: 5.1 us -> 3.78 us  [exchange(): return lax.ppermute(value, axis, pairs)]
  transfers between devices with their start and end apart: 17 -> 17, of which waited for: 3 -> 5; matrix products, arithmetic and copies ran while one was open for 0% -> 0% of each run, Pallas kernels for 34% -> 34%
where the time goes in v4:
time: 71.9 us; the launch traced here: 71.7 us
  Pallas kernels  44.2 us (61%)
  starting transfers between devices  22.2 us (31%)
  waiting for transfers between devices  3.78 us (5%)
  between operations  1.47 us (2%)
    ppermute x17, starting transfers between devices, exchange(): return lax.ppermute(value, axis, pairs)  22.2 us
    pallas_call x2, Pallas kernels, run_load(): pl.pallas_call(functools.partial(load_kernel, first, len(widths)), out_sh...  15.5 us
    pallas_call x2, Pallas kernels, run_update(): pl.pallas_call(functools.partial(update_kernel, n_tp, n_held, len(kept),...  13.3 us
    pallas_call x1, Pallas kernels, run_attention(): pl.pallas_call(functools.partial(attention_kernel, kv_local), out_shape=(...  6.18 us
    pallas_call x1, Pallas kernels, run_logits(): pl.pallas_call(functools.partial(logits_kernel, n_rep, n_tp), grid=(tiles...  4.77 us
    ppermute x17, waiting for transfers between devices, exchange(): return lax.ppermute(value, axis, pairs)  3.78 us
    pallas_call x1, Pallas kernels, run_scale(): pl.pallas_call(functools.partial(scale_kernel, len(helds), first), out_sh...  2.8 us
  transfers between devices with their start and end apart: 17, of which 5 were waited for; matrix products, arithmetic and copies ran while one was open for 0% of the time, Pallas kernels for 34%

profile of v4, /device:TPU:0, one launch (start us, length us, event | category | flops | bytes accessed | tf_op | source)
XLA Modules:
  0.0 71.7 jit_solution(3813729540281498636)
XLA Ops:
  1.3 6.2 %attention.1 = (bf16[16,4096]{1,0:T(8,128)(2,1)S(1)}, bf16[4,4096]{1,0:T(4,128)(2,1)}, f32[4096,512]{1,0:T(8,128)S(1)}) custom-call(s32[16]{0:T(128)} %bitcast.13, s32[1]{0:T(128)S(6)} %copy.38.length_ref, bf16[4,16384]{1,0:T(4,128)(2,1)} %bitcast.11, bf16[16,64,256]{2,1,0:T(8,128)(2,1)} %bitcast.9, bf16[16,64,256]{2,1,0:T(8,128)(2,1)} %bitcast.10, ...), custom_call_target="tpu_custom_call" | custom-call | flops 67108864 | bytes 12582912 | tf_op jit(solution)/shard_map/attention/pallas_call | solution.py:251
  7.5 0.0 copy-start
  7.5 4.0 %collective-permute-start.2 = (bf16[16,4096]{1,0:T(8,128)(2,1)S(1)}, bf16[16,4096]{1,0:T(8,128)(2,1)S(1)}, u32[]{:S(2)}, u32[]{:S(2)}) collective-permute-start(bf16[16,4096]{1,0:T(8,128)(2,1)S(1)} %get-tuple-element.35.token_ref.refs_0_), channel_id=1, source_target_pairs={{0,24},{4,28},{8,16},{12,20},{16,8},{20,12},{24,0},{28,4},{1,25},{... | collective-permute-start | bytes 393224 | tf_op jit(solution)/shard_map/ppermute | solution.py:142
  11.4 0.5 collective-permute-start.1
  11.9 0.1 collective-permute-start
  12.1 5.9 %load_weight.2 = (f32[4096,1024]{1,0:T(8,128)S(1)}, f32[8,128]{1,0:T(8,128)S(1)}) custom-call(f32[4096,2048]{1,0:T(8,128)} %weight_ref.7, bf16[16,4096]{1,0:T(8,128)(2,1)S(1)} %get-tuple-element.35.token_ref.refs_0_), custom_call_target="tpu_custom_call" | custom-call | bytes 16777216 | tf_op jit(solution)/shard_map/load_weight/pallas_call | solution.py:315
  18.1 0.1 collective-permute-start.3
  18.2 1.9 %collective-permute-done.3.refs_1_ = bf16[64,4096]{1,0:T(8,128)(2,1)S(1)} collective-permute-done((bf16[64,4096]{1,0:T(8,128)(2,1)S(1)}, bf16[64,4096]{1,0:T(8,128)(2,1)S(1)}, u32[]{:S(2)}, u32[]{:S(2)}) %collective-permute-start.3) | collective-permute-done | bytes 524320 | tf_op jit(solution)/shard_map/ppermute | solution.py:142
  20.1 4.8 %partial_logits.1 = (bf16[128,4096]{1,0:T(8,128)(2,1)S(1)}, f32[32,2048]{1,0:T(8,128)S(1)}, f32[128,128]{1,0:T(8,128)S(1)}, s16[32,2176]{1,0:T(8,128)(2,1)S(1)},...) custom-call(bf16[64,4096]{1,0:T(8,128)(2,1)S(1)} %stacked_rows.1.refs_0_, ...), custom_call_target="tpu_custom_call" | custom-call | flops 6442450944 | bytes 33554432 | tf_op jit(solution)/shard_map/partial_logits/pallas_call | solution.py:445
  24.8 3.1 %collective-permute-start.4 = (s16[32,2176]{1,0:T(8,128)(2,1)S(1)}, s16[32,2176]{1,0:T(8,128)(2,1)S(1)}, u32[]{:S(2)}, u32[]{:S(2)}) collective-permute-start(s16[32,2176]{1,0:T(8,128)(2,1)S(1)} %get-tuple-element.42), channel_id=1, source_target_pairs={{0,2},{1,3},{2,0},{3,1},{4,6},{5,7},{6,4},{7,5},{8,10},{9,11},{10,... | collective-permute-start | bytes 417800 | tf_op jit(solution)/shard_map/ppermute | solution.py:142
  27.9 1.6 %collective-permute-start.5 = (s16[32,2176]{1,0:T(8,128)(2,1)S(1)}, s16[32,2176]{1,0:T(8,128)(2,1)S(1)}, u32[]{:S(2)}, u32[]{:S(2)}) collective-permute-start(s16[32,2176]{1,0:T(8,128)(2,1)S(1)} %get-tuple-element.43), channel_id=1, source_target_pairs={{0,1},{1,0},{2,3},{3,2},{4,5},{5,4},{6,7},{7,6},{8,9},{9,8},{10,11... | collective-permute-start | bytes 417800 | tf_op jit(solution)/shard_map/ppermute | solution.py:142
  29.5 9.6 %load_weight.3 = (f32[4096,768]{1,0:T(8,128)S(1)}, f32[4096,1024]{1,0:T(8,128)S(1)}, f32[8,128]{1,0:T(8,128)S(1)}) custom-call(f32[4096,2048]{1,0:T(8,128)} %weight_ref.7, f32[32,2048]{1,0:T(8,128)S(1)} %get-tuple-element.40.token_ref.own_ref), custom_call_target="tpu_custom_call" | custom-call | bytes 29360128 | tf_op jit(solution)/shard_map/load_weight/pallas_call | solution.py:315
  39.1 0.0 copy-start.1
  39.1 0.4 local_softmax.1
  39.5 3.9 %collective-permute-start.12 = (bf16[32,896]{1,0:T(8,128)(2,1)S(1)}, bf16[32,896]{1,0:T(8,128)(2,1)S(1)}, u32[]{:S(2)}, u32[]{:S(2)}) collective-permute-start(bf16[32,896]{1,0:T(8,128)(2,1)S(1)} %get-tuple-element.54.refs_0_.refs_2_), channel_id=1, source_target_pairs={{0,3},{1,2},{2,1},{3,0},{4,7},{5,6},{6,5},{7,4},{8,11},{9,10},{10,... | collective-permute-start | bytes 172040 | tf_op jit(solution)/shard_map/ppermute | solution.py:142
  43.4 0.6 collective-permute-start.11
  44.0 0.5 collective-permute-start.10
  44.5 0.9 %turned_rows.1.turned_ref = f32[4096,128]{1,0:T(8,128)S(1)} custom-call(bf16[128,4096]{1,0:T(8,128)(2,1)S(1)} %get-tuple-element.39.x_ref, f32[1,4096]{1,0:T(1,128)S(1)} %bitcast.8), custom_call_target="tpu_custom_call" | custom-call | flops 4096 | bytes 4096 | tf_op jit(solution)/shard_map/turned_rows/pallas_call | solution.py:606
  45.5 2.8 %scaled_rows.1 = (bf16[4096,256]{1,0:T(8,128)(2,1)S(1)}, s32[128,128]{1,0:T(8,128)S(1)}, f32[4096,768]{1,0:T(8,128)S(1)}, f32[4096,1024]{1,0:T(8,128)S(1)}, f32[4096,256]{1,0:T(8,128)S(1)}) custom-call(f32[4096,128]{1,0:T(8,128)S(1)} %turned_rows.1.turned_ref, ...), custom_call_target="tpu_custom_call", output_to_operand_aliasing={{2}: (5, {}), {3}: (6, {})} | custom-call | flops 65536 | bytes 65536 | tf_op jit(solution)/shard_map/scaled_rows/pallas_call | solution.py:650
  48.3 0.3 collective-permute-done.11.refs_2_.refs_4_
  48.6 0.2 collective-permute-done.10.refs_1_.refs_3_
  48.8 0.2 row_stats.1
  49.0 0.0 collective-permute-start.13
  49.1 1.2 %collective-permute-done.13.second_ref = f32[8,128]{1,0:T(8,128)S(1)} collective-permute-done((f32[8,128]{1,0:T(8,128)S(1)}, f32[8,128]{1,0:T(8,128)S(1)}, u32[]{:S(2)}, u32[]{:S(2)}) %collective-permute-start.13) | collective-permute-done | bytes 4128 | tf_op jit(solution)/shard_map/ppermute | solution.py:142
  50.3 2.5 %collective-permute-start.16 = (f32[8,128]{1,0:T(8,128)S(1)}, f32[8,128]{1,0:T(8,128)S(1)}, u32[]{:S(2)}, u32[]{:S(2)}) collective-permute-start(f32[8,128]{1,0:T(8,128)S(1)} %pair_stats.1.refs_7_), channel_id=1, source_target_pairs={{0,24},{4,28},{8,16},{12,20},{16,8},{20,12},{24,0},{28,4},{1,25},{... | collective-permute-start | bytes 12296 | tf_op jit(solution)/shard_map/ppermute | solution.py:142
  52.8 0.5 collective-permute-start.15
  53.3 0.5 collective-permute-start.14
  53.8 3.2 %collective-permute-start.9 = (bf16[32,1280]{1,0:T(8,128)(2,1)S(1)}, bf16[32,1280]{1,0:T(8,128)(2,1)S(1)}, u32[]{:S(2)}, u32[]{:S(2)}) collective-permute-start(bf16[32,1280]{1,0:T(8,128)(2,1)S(1)} %get-tuple-element.53.refs_2_), channel_id=1, source_target_pairs={{0,3},{1,2},{2,1},{3,0},{4,7},{5,6},{6,5},{7,4},{8,11},{9,10},{10,... | collective-permute-start | bytes 245768 | tf_op jit(solution)/shard_map/ppermute | solution.py:142
  57.0 1.2 %collective-permute-start.7 = (bf16[32,1280]{1,0:T(8,128)(2,1)S(1)}, bf16[32,1280]{1,0:T(8,128)(2,1)S(1)}, u32[]{:S(2)}, u32[]{:S(2)}) collective-permute-start(bf16[32,1280]{1,0:T(8,128)(2,1)S(1)} %get-tuple-element.53.refs_2_), channel_id=1, source_target_pairs={{0,1},{1,0},{2,3},{3,2},{4,5},{5,4},{6,7},{7,6},{8,9},{9,8},{10,11... | collective-permute-start | bytes 245768 | tf_op jit(solution)/shard_map/ppermute | solution.py:142
  58.2 5.3 %weight_update.2 = (f32[4096,2048]{1,0:T(8,128)}, f32[4096,768]{1,0:T(8,128)S(1)}, f32[4096,1024]{1,0:T(8,128)S(1)}, f32[4096,256]{1,0:T(8,128)S(1)}) custom-call(bf16[4096,256]{1,0:T(8,128)(2,1)S(1)} %get-tuple-element.51.refs_0_, s32[128,128]{1,0:T(8,128)S(1)} %get-tuple-element.52.refs_1_, ...), custom_call_target="tpu_custom_call", output_to_operand_aliasing={{1}: (11, {}), {2}: (12, {}), {3}: (13, {})} | custom-call | flops 1610612736 | bytes 12582912 | tf_op jit(solution)/shard_map/weight_update/pallas_call | solution.py:742
  63.5 0.2 collective-permute-done.8.refs_4_
  63.7 8.0 %weight_update.3 = (f32[4096,2048]{1,0:T(8,128)}, f32[4096,1024]{1,0:T(8,128)S(1)}, f32[4096,256]{1,0:T(8,128)S(1)}) custom-call(bf16[4096,256]{1,0:T(8,128)(2,1)S(1)} %get-tuple-element.51.refs_0_, s32[128,128]{1,0:T(8,128)S(1)} %get-tuple-element.52.refs_1_, ...), custom_call_target="tpu_custom_call", output_to_operand_aliasing={{1}: (12, {}), {2}: (13, {}), {0}: (11, {})} | custom-call | flops 2684354560 | bytes 20971520 | tf_op jit(solution)/shard_map/weight_update/pallas_call | solution.py:742
  (20 shorter events, 0.1 us)
Async XLA Ops:
  7.5 12.6 %copy-start = (f32[4096]{0:T(1024)S(1)}, f32[4096]{0:T(1024)}, u32[]{:S(2)}) copy-start(f32[4096]{0:T(1024)} %param.16) | copy-start | bytes 49156
  7.5 10.5 %collective-permute-start.2 = (bf16[16,4096]{1,0:T(8,128)(2,1)S(1)}, bf16[16,4096]{1,0:T(8,128)(2,1)S(1)}, u32[]{:S(2)}, u32[]{:S(2)}) collective-permute-start(bf16[16,4096]{1,0:T(8,128)(2,1)S(1)} %get-tuple-element.35.token_ref.refs_0_), channel_id=1, source_target_pairs={{0,24},{4,28},{8,16},{12,20},{16,8},{20,12},{24,0},{28,4},{1,25},{... | collective-permute-start | bytes 393224 | tf_op jit(solution)/shard_map/ppermute | solution.py:142
  11.4 6.6 %collective-permute-start.1 = (bf16[16,4096]{1,0:T(8,128)(2,1)S(1)}, bf16[16,4096]{1,0:T(8,128)(2,1)S(1)}, u32[]{:S(2)}, u32[]{:S(2)}) collective-permute-start(bf16[16,4096]{1,0:T(8,128)(2,1)S(1)} %get-tuple-element.35.token_ref.refs_0_), channel_id=1, source_target_pairs={{0,16},{4,20},{8,24},{12,28},{16,0},{20,4},{24,8},{28,12},{1,17},{... | collective-permute-start | bytes 393224 | tf_op jit(solution)/shard_map/ppermute | solution.py:142
  11.9 6.1 %collective-permute-start = (bf16[16,4096]{1,0:T(8,128)(2,1)S(1)}, bf16[16,4096]{1,0:T(8,128)(2,1)S(1)}, u32[]{:S(2)}, u32[]{:S(2)}) collective-permute-start(bf16[16,4096]{1,0:T(8,128)(2,1)S(1)} %get-tuple-element.35.token_ref.refs_0_), channel_id=1, source_target_pairs={{0,8},{4,12},{8,0},{12,4},{16,24},{20,28},{24,16},{28,20},{1,9},{5... | collective-permute-start | bytes 393224 | tf_op jit(solution)/shard_map/ppermute | solution.py:142
  18.1 2.0 %collective-permute-start.3 = (bf16[64,4096]{1,0:T(8,128)(2,1)S(1)}, bf16[64,4096]{1,0:T(8,128)(2,1)S(1)}, u32[]{:S(2)}, u32[]{:S(2)}) collective-permute-start(bf16[64,4096]{1,0:T(8,128)(2,1)S(1)} %stacked_rows.1.refs_0_), channel_id=1, source_target_pairs={{0,4},{4,0},{8,12},{12,8},{16,20},{20,16},{24,28},{28,24},{1,5},{5... | collective-permute-start | bytes 1572872 | tf_op jit(solution)/shard_map/ppermute | solution.py:142
  24.8 14.2 %collective-permute-start.4 = (s16[32,2176]{1,0:T(8,128)(2,1)S(1)}, s16[32,2176]{1,0:T(8,128)(2,1)S(1)}, u32[]{:S(2)}, u32[]{:S(2)}) collective-permute-start(s16[32,2176]{1,0:T(8,128)(2,1)S(1)} %get-tuple-element.42), channel_id=1, source_target_pairs={{0,2},{1,3},{2,0},{3,1},{4,6},{5,7},{6,4},{7,5},{8,10},{9,11},{10,... | collective-permute-start | bytes 417800 | tf_op jit(solution)/shard_map/ppermute | solution.py:142
  27.9 11.2 %collective-permute-start.5 = (s16[32,2176]{1,0:T(8,128)(2,1)S(1)}, s16[32,2176]{1,0:T(8,128)(2,1)S(1)}, u32[]{:S(2)}, u32[]{:S(2)}) collective-permute-start(s16[32,2176]{1,0:T(8,128)(2,1)S(1)} %get-tuple-element.43), channel_id=1, source_target_pairs={{0,1},{1,0},{2,3},{3,2},{4,5},{5,4},{6,7},{7,6},{8,9},{9,8},{10,11... | collective-permute-start | bytes 417800 | tf_op jit(solution)/shard_map/ppermute | solution.py:142
  29.5 9.6 %collective-permute-start.6 = (s16[32,2176]{1,0:T(8,128)(2,1)S(1)}, s16[32,2176]{1,0:T(8,128)(2,1)S(1)}, u32[]{:S(2)}, u32[]{:S(2)}) collective-permute-start(s16[32,2176]{1,0:T(8,128)(2,1)S(1)} %get-tuple-element.44), channel_id=1, source_target_pairs={{0,3},{1,2},{2,1},{3,0},{4,7},{5,6},{6,5},{7,4},{8,11},{9,10},{10,... | collective-permute-start | bytes 417800 | tf_op jit(solution)/shard_map/ppermute | solution.py:142
  39.1 6.3 %copy-start.1 = (s32[8,16]{1,0:T(8,128)S(1)}, s32[8,16]{1,0:T(8,128)}, u32[]{:S(2)}) copy-start(s32[8,16]{1,0:T(8,128)} %targets_ref.1) | copy-start | bytes 1540
  39.1 6.3 %copy-start.2 = (s32[8]{0:T(128)S(1)}, s32[8]{0:T(128)}, u32[]{:S(2)}) copy-start(s32[8]{0:T(128)} %accepted_ref.1) | copy-start | bytes 100
  39.5 8.7 %collective-permute-start.12 = (bf16[32,896]{1,0:T(8,128)(2,1)S(1)}, bf16[32,896]{1,0:T(8,128)(2,1)S(1)}, u32[]{:S(2)}, u32[]{:S(2)}) collective-permute-start(bf16[32,896]{1,0:T(8,128)(2,1)S(1)} %get-tuple-element.54.refs_0_.refs_2_), channel_id=1, source_target_pairs={{0,3},{1,2},{2,1},{3,0},{4,7},{5,6},{6,5},{7,4},{8,11},{9,10},{10,... | collective-permute-start | bytes 172040 | tf_op jit(solution)/shard_map/ppermute | solution.py:142
  43.4 5.2 %collective-permute-start.11 = (bf16[32,896]{1,0:T(8,128)(2,1)S(1)}, bf16[32,896]{1,0:T(8,128)(2,1)S(1)}, u32[]{:S(2)}, u32[]{:S(2)}) collective-permute-start(bf16[32,896]{1,0:T(8,128)(2,1)S(1)} %get-tuple-element.54.refs_0_.refs_2_), channel_id=1, source_target_pairs={{0,2},{1,3},{2,0},{3,1},{4,6},{5,7},{6,4},{7,5},{8,10},{9,11},{10,... | collective-permute-start | bytes 172040 | tf_op jit(solution)/shard_map/ppermute | solution.py:142
  44.0 4.8 %collective-permute-start.10 = (bf16[32,896]{1,0:T(8,128)(2,1)S(1)}, bf16[32,896]{1,0:T(8,128)(2,1)S(1)}, u32[]{:S(2)}, u32[]{:S(2)}) collective-permute-start(bf16[32,896]{1,0:T(8,128)(2,1)S(1)} %get-tuple-element.54.refs_0_.refs_2_), channel_id=1, source_target_pairs={{0,1},{1,0},{2,3},{3,2},{4,5},{5,4},{6,7},{7,6},{8,9},{9,8},{10,11... | collective-permute-start | bytes 172040 | tf_op jit(solution)/shard_map/ppermute | solution.py:142
  49.0 1.2 %collective-permute-start.13 = (f32[8,128]{1,0:T(8,128)S(1)}, f32[8,128]{1,0:T(8,128)S(1)}, u32[]{:S(2)}, u32[]{:S(2)}) collective-permute-start(f32[8,128]{1,0:T(8,128)S(1)} %get-tuple-element.58.first_ref.refs_6_), channel_id=1, source_target_pairs={{0,4},{4,0},{8,12},{12,8},{16,20},{20,16},{24,28},{28,24},{1,5},{5... | collective-permute-start | bytes 12296 | tf_op jit(solution)/shard_map/ppermute | solution.py:142
  50.3 6.8 %collective-permute-start.16 = (f32[8,128]{1,0:T(8,128)S(1)}, f32[8,128]{1,0:T(8,128)S(1)}, u32[]{:S(2)}, u32[]{:S(2)}) collective-permute-start(f32[8,128]{1,0:T(8,128)S(1)} %pair_stats.1.refs_7_), channel_id=1, source_target_pairs={{0,24},{4,28},{8,16},{12,20},{16,8},{20,12},{24,0},{28,4},{1,25},{... | collective-permute-start | bytes 12296 | tf_op jit(solution)/shard_map/ppermute | solution.py:142
  52.8 5.4 %collective-permute-start.15 = (f32[8,128]{1,0:T(8,128)S(1)}, f32[8,128]{1,0:T(8,128)S(1)}, u32[]{:S(2)}, u32[]{:S(2)}) collective-permute-start(f32[8,128]{1,0:T(8,128)S(1)} %pair_stats.1.refs_7_), channel_id=1, source_target_pairs={{0,16},{4,20},{8,24},{12,28},{16,0},{20,4},{24,8},{28,12},{1,17},{... | collective-permute-start | bytes 12296 | tf_op jit(solution)/shard_map/ppermute | solution.py:142
  53.3 4.9 %collective-permute-start.14 = (f32[8,128]{1,0:T(8,128)S(1)}, f32[8,128]{1,0:T(8,128)S(1)}, u32[]{:S(2)}, u32[]{:S(2)}) collective-permute-start(f32[8,128]{1,0:T(8,128)S(1)} %pair_stats.1.refs_7_), channel_id=1, source_target_pairs={{0,8},{4,12},{8,0},{12,4},{16,24},{20,28},{24,16},{28,20},{1,9},{5... | collective-permute-start | bytes 12296 | tf_op jit(solution)/shard_map/ppermute | solution.py:142
  53.8 9.7 %collective-permute-start.9 = (bf16[32,1280]{1,0:T(8,128)(2,1)S(1)}, bf16[32,1280]{1,0:T(8,128)(2,1)S(1)}, u32[]{:S(2)}, u32[]{:S(2)}) collective-permute-start(bf16[32,1280]{1,0:T(8,128)(2,1)S(1)} %get-tuple-element.53.refs_2_), channel_id=1, source_target_pairs={{0,3},{1,2},{2,1},{3,0},{4,7},{5,6},{6,5},{7,4},{8,11},{9,10},{10,... | collective-permute-start | bytes 245768 | tf_op jit(solution)/shard_map/ppermute | solution.py:142
  57.0 6.6 %collective-permute-start.8 = (bf16[32,1280]{1,0:T(8,128)(2,1)S(1)}, bf16[32,1280]{1,0:T(8,128)(2,1)S(1)}, u32[]{:S(2)}, u32[]{:S(2)}) collective-permute-start(bf16[32,1280]{1,0:T(8,128)(2,1)S(1)} %get-tuple-element.53.refs_2_), channel_id=1, source_target_pairs={{0,2},{1,3},{2,0},{3,1},{4,6},{5,7},{6,4},{7,5},{8,10},{9,11},{10,... | collective-permute-start | bytes 245768 | tf_op jit(solution)/shard_map/ppermute | solution.py:142
  57.0 6.6 %collective-permute-start.7 = (bf16[32,1280]{1,0:T(8,128)(2,1)S(1)}, bf16[32,1280]{1,0:T(8,128)(2,1)S(1)}, u32[]{:S(2)}, u32[]{:S(2)}) collective-permute-start(bf16[32,1280]{1,0:T(8,128)(2,1)S(1)} %get-tuple-element.53.refs_2_), channel_id=1, source_target_pairs={{0,1},{1,0},{2,3},{3,2},{4,5},{5,4},{6,7},{7,6},{8,9},{9,8},{10,11... | collective-permute-start | bytes 245768 | tf_op jit(solution)/shard_map/ppermute | solution.py:142
